TPU v7x, 512 devices: a whole 4x8x8 slice. The times are simulated.
512 devices in a mesh: gx: 32 (over y, z_lo), gy: 4 (over z_hi, core), sp: 4 (over x).
Axes of the slice: x: 4, y: 8, z: 8 (z_hi: 2, z_lo: 4; z = z_hi * 4 + z_lo), core: 2. Of those that a mesh axis runs over, the one named last changes fastest.
Arguments:
- latent: float32 [16, 512, 2048], P(None, 'gx', 'gy'), may hold values from -2 to 2
- kappa_sq: float32 [16, 512, 2048], P('sp', 'gx', 'gy'), may hold values from 0.05 to 3
- coefs: float32 [128, 512, 2048], P('sp', 'gx', 'gy'), may hold values from -1.5 to 0.5
- loadings: float32 [128, 16], P('sp'), may hold values from -1.5 to 1.5
- counts: int32 [128, 512, 2048], P('sp', 'gx', 'gy'), may hold values from 0 to 4
- land: int32 [512, 2048], P('gx', 'gy'), may hold values 0 or 1
Outputs:
- grad_latent: float32 [16, 512, 2048], P('sp', 'gx', 'gy')
- grad_loadings: float32 [128, 16], P('sp')
All inputs are finite; a program needn't handle non-finite values. No bound on the sum of `land` on one device may be relied on, other than what follows from the above.
Results may differ from a plain program's by a relative error of at most 0.000068.
Values sent between devices are 32-bit elements; how exact they have to be, the bound alone decides.
No kernel may reach another device: no remote copies, remote signals or barrier semaphores. Data moves between devices by JAX's collectives and lax.ppermute only.
A program may use at most 64 MiB of HBM per device.

v0:
```python
import jax
import jax.numpy as jnp
from jax import lax
from jax.sharding import PartitionSpec as P


def extended(cells, sides, width):
    for axis, dim in sides:
        count = lax.axis_size(axis)
        ends = count - 1
        head = lax.slice_in_dim(cells, 0, width, axis=dim)
        tail = lax.slice_in_dim(cells, cells.shape[dim] - width, cells.shape[dim], axis=dim)
        cells = jnp.concatenate(
            [
                lax.ppermute(tail, axis, [(i, (i + 1) % count) for i in range(ends)]),
                cells,
                lax.ppermute(head, axis, [((i + 1) % count, i) for i in range(ends)]),
            ],
            axis=dim,
        )
    return cells


def stencil(padded, kappa):
    beside = padded[:, 2:, 1:-1] + padded[:, :-2, 1:-1] + padded[:, 1:-1, 2:] + padded[:, 1:-1, :-2]
    return (kappa + 4.0) * padded[:, 1:-1, 1:-1] - beside


def loading_total(local_sums):
    return lax.psum(local_sums, ("gx", "gy"))


def per_device(latent, kappa_sq, coefs, loadings, counts, land):
    highest = lax.Precision.HIGHEST
    fields_own = kappa_sq.shape[0]
    rows, cols = land.shape
    mix = jnp.einsum("sk,kxy->sxy", loadings, latent, precision=highest)
    resid = land.astype(jnp.float32)[None] * (counts.astype(jnp.float32) - jnp.exp(coefs + mix))
    local_sums = jnp.einsum("sxy,kxy->sk", resid, latent, precision=highest)
    scale = 1.0 / jnp.sqrt(jnp.float32(rows * lax.axis_size("gx") * cols * lax.axis_size("gy")))
    own_fields = lax.dynamic_slice_in_dim(latent, lax.axis_index("sp") * fields_own, fields_own, 0)
    field_padded = extended(own_fields, (("gx", 1), ("gy", 2)), 1)
    first = stencil(field_padded, kappa_sq)
    first_padded = extended(first, (("gx", 1), ("gy", 2)), 1)
    prior_part = stencil(first_padded, kappa_sq)
    species_part = lax.psum_scatter(
        jnp.einsum("sk,sxy->kxy", loadings, resid, precision=highest),
        "sp",
        scatter_dimension=0,
        tiled=True,
    )
    grad_latent = species_part - prior_part
    totals = loading_total(local_sums)
    return (grad_latent, totals * scale)


def solution(mesh):
    return jax.shard_map(
        per_device,
        mesh=mesh,
        in_specs=(
            P(None, "gx", "gy"),
            P("sp", "gx", "gy"),
            P("sp", "gx", "gy"),
            P("sp", None),
            P("sp", "gx", "gy"),
            P("gx", "gy"),
        ),
        out_specs=(P("sp", "gx", "gy"), P("sp", None)),
        check_vma=False,
    )
```

profile of v0, /device:TPU:37, one launch (start us, length us, event | category | flops | bytes accessed | tf_op | source)
XLA Modules:
  0.0 340.0 jit_solution(10901677016360641042)
XLA Ops:
  7.2 0.0 copy-start
  7.2 0.0 copy-start.3
  7.2 0.0 reduce-scatter.2.cloned.1.call-start
  7.2 0.9 constant_dynamic-slice_fusion
  8.1 4.0 %collective-permute-start.1 = (f32[4,1,512]{2,1,0:T(1,128)S(1)}, f32[4,1,512]{2,1,0:T(1,128)S(1)}, u32[]{:S(2)}, u32[]{:S(2)}) collective-permute-start(f32[4,1,512]{2,1,0:T(1,128)S(1)} %get-tuple-element.4), channel_id=1, source_target_pairs={{0,16},{16,32},{32,48},{48,64},{64,80},{80,96},{96,112},{112,128},... | collective-permute-start | bytes 24584 | tf_op jit(solution)/shard_map/ppermute | solution.py:15
  12.1 5.4 %collective-permute-start = (f32[4,1,512]{2,1,0:T(1,128)S(1)}, f32[4,1,512]{2,1,0:T(1,128)S(1)}, u32[]{:S(2)}, u32[]{:S(2)}) collective-permute-start(f32[4,1,512]{2,1,0:T(1,128)S(1)} %get-tuple-element.5), channel_id=1, source_target_pairs={{16,0},{32,16},{48,32},{64,48},{80,64},{96,80},{112,96},{128,112},... | collective-permute-start | bytes 24584 | tf_op jit(solution)/shard_map/ppermute | solution.py:17
  17.6 0.0 copy-done.3
  17.6 0.0 copy-done
  17.6 4.0 %fusion.2 = f32[32,16,512]{2,0,1:T(8,128)S(1)} fusion(f32[32,16,512]{2,1,0:T(8,128)} %param.8, s32[32,16,512]{2,1,0:T(8,128)} %param.10, f32[16,512]{1,0:T(8,128)S(1)} %convert_element_type.6, f32[16,16,512]{2,1,0:T(8,128)} %param.6, f32[32,16]{0,1:T(8,128)S(1)} %copy-done), kind=kOutput, calls=%fused_computation.3 | convolution fusion | flops 51380224 | bytes 3704832 | tf_op jit(solution)/shard_map/sk,kxy->sxy/dot_general | solution.py:37
  21.6 0.7 convolution_bitcast_fusion
  22.3 1.1 copy.18
  23.4 0.0 copy-start.1
  23.4 0.0 reduce-scatter.2.cloned.1.call-update
  23.4 1.0 copy-done.1
  24.5 0.0 copy-start.2
  24.5 0.0 collective-permute-done.1
  24.5 0.0 collective-permute-done
  24.5 0.1 pad_maximum_fusion.21
  24.6 2.9 collective-permute-start.2
  27.5 10.5 %collective-permute-start.3 = (f32[4,18,1]{2,1,0:T(8,128)S(1)}, f32[4,18,1]{2,1,0:T(8,128)S(1)}, u32[]{:S(2)}, u32[]{:S(2)}) collective-permute-start(f32[4,18,1]{2,1,0:T(8,128)S(1)} %get-tuple-element.9), channel_id=1, source_target_pairs={{0,4},{4,8},{8,12},{1,5},{5,9},{9,13},{2,6},{6,10},{10,14},{3,7},{... | collective-permute-start | bytes 872 | tf_op jit(solution)/shard_map/ppermute | solution.py:15
  38.0 0.0 collective-permute-done.2
  38.1 1.1 collective-permute-done.3
  39.2 0.0 copy-done.2
  39.2 0.2 fusion.11
  39.4 1.9 collective-permute-start.5
  41.3 7.3 %collective-permute-start.4 = (f32[4,1,512]{2,1,0:T(1,128)S(1)}, f32[4,1,512]{2,1,0:T(1,128)S(1)}, u32[]{:S(2)}, u32[]{:S(2)}) collective-permute-start(f32[4,1,512]{2,1,0:T(1,128)S(1)} %get-tuple-element.11), channel_id=1, source_target_pairs={{16,0},{32,16},{48,32},{64,48},{80,64},{96,80},{112,96},{128,112},... | collective-permute-start | bytes 24584 | tf_op jit(solution)/shard_map/ppermute | solution.py:17
  48.6 1.1 convolution_bitcast_fusion.1
  49.7 270.3 %psum.7 = f32[32,16]{0,1:T(8,128)S(1)} all-reduce(f32[32,16]{0,1:T(8,128)S(1)} %convolution_bitcast_fusion.1), channel_id=1, replica_groups=mesh['gx'=32,'gy'=4,'sp'=4] {'gx','gy'}, use_global_device_ids=true, to_apply=%region_1.0 | all-reduce | flops 512 | bytes 4096 | tf_op jit(solution)/shard_map/psum | solution.py:30
  320.1 0.0 collective-permute-done.5
  320.1 0.0 collective-permute-done.4
  320.1 0.1 pad_maximum_fusion.18
  320.2 1.9 collective-permute-start.6
  322.1 8.1 %collective-permute-start.7 = (f32[4,18,1]{2,1,0:T(8,128)S(1)}, f32[4,18,1]{2,1,0:T(8,128)S(1)}, u32[]{:S(2)}, u32[]{:S(2)}) collective-permute-start(f32[4,18,1]{2,1,0:T(8,128)S(1)} %get-tuple-element.7), channel_id=1, source_target_pairs={{0,4},{4,8},{8,12},{1,5},{5,9},{9,13},{2,6},{6,10},{10,14},{3,7},{... | collective-permute-start | bytes 872 | tf_op jit(solution)/shard_map/ppermute | solution.py:15
  330.2 0.6 broadcast_multiply_fusion
  330.8 0.0 collective-permute-done.6
  330.8 0.6 collective-permute-done.7
  331.4 0.0 reduce-scatter.2.cloned.1.call-done
  331.4 1.7 fusion.7
  (3 shorter events, 0.0 us)
Async XLA Ops:
  7.2 10.4 %copy-start = (f32[32,16]{0,1:T(8,128)S(1)}, f32[32,16]{0,1:T(8,128)}, u32[]{:S(2)}) copy-start(f32[32,16]{0,1:T(8,128)} %param.9) | copy-start | bytes 6148
  7.2 10.4 %copy-start.3 = (s32[16,512]{1,0:T(8,128)S(1)}, s32[16,512]{1,0:T(8,128)}, u32[]{:S(2)}) copy-start(s32[16,512]{1,0:T(8,128)} %param.11) | copy-start | bytes 98308
  7.2 324.2 %reduce-scatter.2.cloned.1.call-start = ((), (), s32[]{:S(2)}) async-start(), calls=%async_computation.1 | async-start | bytes 655360 | tf_op jit(solution)/shard_map/reduce_scatter | solution.py:46
  8.1 16.3 %collective-permute-start.1 = (f32[4,1,512]{2,1,0:T(1,128)S(1)}, f32[4,1,512]{2,1,0:T(1,128)S(1)}, u32[]{:S(2)}, u32[]{:S(2)}) collective-permute-start(f32[4,1,512]{2,1,0:T(1,128)S(1)} %get-tuple-element.4), channel_id=1, source_target_pairs={{0,16},{16,32},{32,48},{48,64},{64,80},{80,96},{96,112},{112,128},... | collective-permute-start | bytes 24584 | tf_op jit(solution)/shard_map/ppermute | solution.py:15
  12.1 12.3 %collective-permute-start = (f32[4,1,512]{2,1,0:T(1,128)S(1)}, f32[4,1,512]{2,1,0:T(1,128)S(1)}, u32[]{:S(2)}, u32[]{:S(2)}) collective-permute-start(f32[4,1,512]{2,1,0:T(1,128)S(1)} %get-tuple-element.5), channel_id=1, source_target_pairs={{16,0},{32,16},{48,32},{64,48},{80,64},{96,80},{112,96},{128,112},... | collective-permute-start | bytes 24584 | tf_op jit(solution)/shard_map/ppermute | solution.py:17
  23.4 1.0 copy-start.1
  24.5 14.7 %copy-start.2 = (f32[4,16,512]{2,1,0:T(8,128)S(1)}, f32[4,16,512]{2,1,0:T(8,128)}, u32[]{:S(2)}) copy-start(f32[4,16,512]{2,1,0:T(8,128)} %param.7) | copy-start | bytes 393220
  24.6 13.5 %collective-permute-start.2 = (f32[4,18,1]{2,1,0:T(8,128)S(1)}, f32[4,18,1]{2,1,0:T(8,128)S(1)}, u32[]{:S(2)}, u32[]{:S(2)}) collective-permute-start(f32[4,18,1]{2,1,0:T(8,128)S(1)} %get-tuple-element.8), channel_id=1, source_target_pairs={{4,0},{8,4},{12,8},{5,1},{9,5},{13,9},{6,2},{10,6},{14,10},{7,3},{... | collective-permute-start | bytes 872 | tf_op jit(solution)/shard_map/ppermute | solution.py:17
  27.5 11.7 %collective-permute-start.3 = (f32[4,18,1]{2,1,0:T(8,128)S(1)}, f32[4,18,1]{2,1,0:T(8,128)S(1)}, u32[]{:S(2)}, u32[]{:S(2)}) collective-permute-start(f32[4,18,1]{2,1,0:T(8,128)S(1)} %get-tuple-element.9), channel_id=1, source_target_pairs={{0,4},{4,8},{8,12},{1,5},{5,9},{9,13},{2,6},{6,10},{10,14},{3,7},{... | collective-permute-start | bytes 872 | tf_op jit(solution)/shard_map/ppermute | solution.py:15
  39.4 280.7 %collective-permute-start.5 = (f32[4,1,512]{2,1,0:T(1,128)S(1)}, f32[4,1,512]{2,1,0:T(1,128)S(1)}, u32[]{:S(2)}, u32[]{:S(2)}) collective-permute-start(f32[4,1,512]{2,1,0:T(1,128)S(1)} %get-tuple-element.10), channel_id=1, source_target_pairs={{0,16},{16,32},{32,48},{48,64},{64,80},{80,96},{96,112},{112,128},... | collective-permute-start | bytes 24584 | tf_op jit(solution)/shard_map/ppermute | solution.py:15
  41.3 278.8 %collective-permute-start.4 = (f32[4,1,512]{2,1,0:T(1,128)S(1)}, f32[4,1,512]{2,1,0:T(1,128)S(1)}, u32[]{:S(2)}, u32[]{:S(2)}) collective-permute-start(f32[4,1,512]{2,1,0:T(1,128)S(1)} %get-tuple-element.11), channel_id=1, source_target_pairs={{16,0},{32,16},{48,32},{64,48},{80,64},{96,80},{112,96},{128,112},... | collective-permute-start | bytes 24584 | tf_op jit(solution)/shard_map/ppermute | solution.py:17
  320.2 10.6 %collective-permute-start.6 = (f32[4,18,1]{2,1,0:T(8,128)S(1)}, f32[4,18,1]{2,1,0:T(8,128)S(1)}, u32[]{:S(2)}, u32[]{:S(2)}) collective-permute-start(f32[4,18,1]{2,1,0:T(8,128)S(1)} %get-tuple-element.6), channel_id=1, source_target_pairs={{4,0},{8,4},{12,8},{5,1},{9,5},{13,9},{6,2},{10,6},{14,10},{7,3},{... | collective-permute-start | bytes 872 | tf_op jit(solution)/shard_map/ppermute | solution.py:17
  322.1 9.3 %collective-permute-start.7 = (f32[4,18,1]{2,1,0:T(8,128)S(1)}, f32[4,18,1]{2,1,0:T(8,128)S(1)}, u32[]{:S(2)}, u32[]{:S(2)}) collective-permute-start(f32[4,18,1]{2,1,0:T(8,128)S(1)} %get-tuple-element.7), channel_id=1, source_target_pairs={{0,4},{4,8},{8,12},{1,5},{5,9},{9,13},{2,6},{6,10},{10,14},{3,7},{... | collective-permute-start | bytes 872 | tf_op jit(solution)/shard_map/ppermute | solution.py:15
Sparse Core Ops, SparseCore 0:
  23.5 28.3 reduce-scatter.1
where the time goes:
time: 340 us
  blocking collectives  270 us (79%)
  starting transfers between devices  42.1 us (12%)
  between operations  14.2 us (4%)
  matrix products  5.79 us (2%)
    psum x1, blocking collectives, loading_total(): return lax.psum(local_sums, ('gx', 'gy'))  270 us
    ppermute x4, starting transfers between devices, extended(): lax.ppermute(tail, axis, [(i, (i + 1) % count) for i in range(ends)])  24.6 us
    ppermute x4, starting transfers between devices, extended(): lax.ppermute(head, axis, [((i + 1) % count, i) for i in range(ends)])  17.5 us
  transfers between devices with their start and end apart: 9, of which 2 were waited for; matrix products, arithmetic and copies ran while one was open for 2% of the time, Pallas kernels for 0%

commit v1 on v0

v1 whole, which is shorter than its diff:
```python
import functools
import math

import jax
import jax.numpy as jnp
from jax import lax
from jax.experimental import pallas as pl
from jax.experimental.pallas import tpu as pltpu
from jax.sharding import PartitionSpec as P

HIGHEST = lax.Precision.HIGHEST
TILE = 8
LANES = 128


def iota(shape, dim):
    return lax.broadcasted_iota(jnp.int32, shape, dim)


def dot(a, b, contract):
    return lax.dot_general(a, b, (contract, ((), ())), precision=HIGHEST, preferred_element_type=jnp.float32)


def operator(field, kappa, above, below, left, right):
    rows, cols = field.shape
    row, col = iota(field.shape, 0), iota(field.shape, 1)
    up = jnp.where(row == 0, above, pltpu.roll(field, 1, 0))
    down = jnp.where(row == rows - 1, below, pltpu.roll(field, rows - 1, 0))
    west = jnp.where(col == 0, left, pltpu.roll(field, 1, 1))
    east = jnp.where(col == cols - 1, right, pltpu.roll(field, cols - 1, 1))
    return (kappa + 4.0) * field - ((down + up) + (east + west))


def column_to_row(column, offset):
    shape = (column.shape[0], LANES)
    placed = jnp.where(iota(shape, 1) == iota(shape, 0) + offset, column, 0.0)
    return jnp.sum(placed, axis=0, keepdims=True)


def row_to_column(row, count, offset):
    shape = (count, LANES)
    placed = jnp.where(iota(shape, 1) == iota(shape, 0) + offset, row, 0.0)
    return jnp.sum(placed, axis=1, keepdims=True)


def local_kernel(
    steps, peers, across,
    place_ref, loadings_ref, latent_ref, kappa_ref, coefs_ref, counts_ref, land_ref,
    blocks_ref, own_ref, once_ref, head_ref, tail_ref, *rest,
):
    part_refs, (wide_ref, tall_ref, gram_ref, species_ref) = rest[:-4], rest[-4:]
    step = pl.program_id(0)
    fields, species = loadings_ref.shape
    groups = len(part_refs)
    held = fields // groups
    sp, gy = place_ref[0], place_ref[1]
    cols = latent_ref.shape[2]
    flat_fields, flat_species = fields * TILE, species * TILE

    @pl.when(step == 0)
    def _():
        transposed = loadings_ref[...]
        spread = jnp.where(iota((fields, flat_fields), 1) // TILE == iota((fields, flat_fields), 0), 1.0, 0.0)
        wide = dot(transposed, spread, ((0,), (0,)))
        wide = jnp.broadcast_to(wide[:, None, :], (species, TILE, flat_fields)).reshape(flat_species, flat_fields)
        same = iota(wide.shape, 0) % TILE == iota(wide.shape, 1) % TILE
        wide_ref[...] = jnp.where(same, wide, 0.0)
        spread = jnp.where(iota((species, flat_species), 1) // TILE == iota((species, flat_species), 0), 1.0, 0.0)
        tall = dot(transposed, spread, ((1,), (0,)))
        tall = jnp.broadcast_to(tall[:, None, :], (fields, TILE, flat_species)).reshape(flat_fields, flat_species)
        same = iota(tall.shape, 0) % TILE == iota(tall.shape, 1) % TILE
        tall_ref[...] = jnp.where(same, tall, 0.0)

    latent = latent_ref[...].reshape(flat_fields, cols)
    mix = dot(wide_ref[...], latent, ((1,), (0,)))
    rate = jnp.exp(coefs_ref[...].reshape(flat_species, cols) + mix)
    counts = counts_ref[...].reshape(flat_species, cols).astype(jnp.float32)
    land = jnp.broadcast_to(land_ref[...].astype(jnp.float32)[None], (species, TILE, cols))
    resid = land.reshape(flat_species, cols) * (counts - rate)
    gram = dot(resid, latent, ((1,), (1,)))
    species_ref[...] = dot(tall_ref[...], resid, ((1,), (0,))).reshape(fields, TILE, cols)
    at = pl.ds(pl.multiple_of(step * TILE, TILE), TILE)
    for distance, part_ref in enumerate(part_refs):
        owner = lax.rem(sp + distance, groups)
        part_ref[:, at, :] = species_ref[pl.ds(owner * held, held)]
    own_ref[:, at, :] = latent_ref[pl.ds(sp * held, held)]

    @pl.when(step == 0)
    def _():
        gram_ref[...] = gram

    @pl.when(step > 0)
    def _():
        gram_ref[...] += gram

    @pl.when(step == steps - 1)
    def _():
        for k in range(held):
            own = own_ref[k]
            once = operator(own, kappa_ref[k], 0.0, 0.0, 0.0, 0.0)
            once_ref[k] = once
            head_ref[k] = jnp.concatenate([own[:1], once[:1]], axis=0)
            tail_ref[k] = jnp.concatenate([own[-1:], once[-1:]], axis=0)
        total = gram_ref[...]
        same = iota(total.shape, 0) % TILE == iota(total.shape, 1) % TILE
        total = jnp.sum(jnp.where(same, total, 0.0).reshape(species, TILE, flat_fields), axis=1)
        spread = jnp.where(iota((fields, flat_fields), 1) // TILE == iota((fields, flat_fields), 0), 1.0, 0.0)
        total = dot(spread, total, ((1,), (1,)))
        rim = own_ref.shape[1] * held
        west = column_to_row(own_ref[:, :, :1].reshape(rim, 1), 0) + column_to_row(once_ref[:, :, :1].reshape(rim, 1), rim)
        east = column_to_row(own_ref[:, :, cols - 1:].reshape(rim, 1), 0) + column_to_row(once_ref[:, :, cols - 1:].reshape(rim, 1), rim)
        per_row = LANES // species
        sums = fields // per_row
        pieces = [total[q * sums:(q + 1) * sums] for q in range(per_row)]
        packed = jnp.concatenate(pieces, axis=1)
        for peer in range(peers):
            blocks_ref[peer, :sums] = packed[:, None, :]
            blocks_ref[peer, sums] = jnp.where(peer % across < gy, west, east)


def final_kernel(
    scale, down_count, across,
    place_ref, blocks_ref, own_ref, once_ref, kappa_ref, above_ref, below_ref, *rest,
):
    part_refs, (latent_ref, loadings_ref) = rest[:-2], rest[-2:]
    gy, gx = place_ref[1], place_ref[2]
    held, rows, cols = own_ref.shape
    fields, species = loadings_ref.shape
    per_row = LANES // species
    sums = fields // per_row
    for r in range(sums):
        total = jnp.sum(blocks_ref[:, r, :, :], axis=0) * scale
        for q in range(per_row):
            loadings_ref[q * sums + r:q * sums + r + 1, :] = total[:, q * species:(q + 1) * species]

    rim = held * rows
    north, south = jnp.maximum(gx - 1, 0), jnp.minimum(gx + 1, down_count - 1)
    westward, eastward = jnp.maximum(gy - 1, 0), jnp.minimum(gy + 1, across - 1)
    has_north = jnp.where(gx > 0, 1.0, 0.0)
    has_south = jnp.where(gx < down_count - 1, 1.0, 0.0)
    has_west = jnp.where(gy > 0, 1.0, 0.0)
    has_east = jnp.where(gy < across - 1, 1.0, 0.0)

    def halo(i, j):
        return blocks_ref[i * across + j, sums]

    lane = iota((1, LANES), 1)

    def column(j, present):
        middle, upper, lower = halo(gx, j), halo(north, j) * has_north, halo(south, j) * has_south
        first = (lane >= rim) & (lane % rows == 0)
        last = (lane >= rim) & (lane % rows == rows - 1)
        middle = middle - jnp.where(first, pltpu.roll(upper, rim - (rows - 1), 1), 0.0)
        middle = middle - jnp.where(last, pltpu.roll(lower, rim + (rows - 1), 1), 0.0)
        middle = middle * present
        return row_to_column(middle, rim, 0), row_to_column(middle, rim, rim), upper * present, lower * present

    west, west_once, north_west, south_west = column(westward, has_west)
    east, east_once, north_east, south_east = column(eastward, has_east)
    for k in range(held):
        own, kappa = own_ref[k], kappa_ref[k]
        span = slice(k * rows, (k + 1) * rows)
        row, col = iota(own.shape, 0), iota(own.shape, 1)
        once = once_ref[k]
        once = once - jnp.where(row == 0, above_ref[k, :1], 0.0) - jnp.where(row == rows - 1, below_ref[k, :1], 0.0)
        once = once - jnp.where(col == 0, west[span], 0.0) - jnp.where(col == cols - 1, east[span], 0.0)
        edge = iota((1, cols), 1)

        def beside(sent, mine, left, right, at, present):
            corner = k * rows + at
            corners = jnp.where(edge == 0, left[:, corner:corner + 1], 0.0) + jnp.where(edge == cols - 1, right[:, corner:corner + 1], 0.0)
            return (sent - mine - corners) * present

        above = beside(above_ref[k, 1:], own[:1], north_west, north_east, rows - 1, has_north)
        below = beside(below_ref[k, 1:], own[rows - 1:], south_west, south_east, 0, has_south)
        left = (west_once[span] - own[:, :1]) * has_west
        right = (east_once[span] - own[:, cols - 1:]) * has_east
        prior = operator(once, kappa, above, below, left, right)
        species_sum = part_refs[0][k]
        for part_ref in part_refs[1:]:
            species_sum = species_sum + part_ref[k]
        latent_ref[k] = species_sum - prior


def per_device(latent, kappa_sq, coefs, loadings, counts, land):
    fields, rows, cols = latent.shape
    species = loadings.shape[0]
    held = kappa_sq.shape[0]
    down_count, across, groups = lax.axis_size("gx"), lax.axis_size("gy"), lax.axis_size("sp")
    peers = down_count * across
    steps = rows // TILE
    lines = fields * species // LANES + 1
    flat_fields, flat_species = fields * TILE, species * TILE
    f32 = jnp.float32
    place = jnp.stack([lax.axis_index("sp"), lax.axis_index("gy"), lax.axis_index("gx")]).astype(jnp.int32)
    whole = lambda *shape: pl.BlockSpec(shape, lambda t: (0,) * len(shape))
    by_rows = lambda count: pl.BlockSpec((count, TILE, cols), lambda t: (0, t, 0))
    field_block = jax.ShapeDtypeStruct((held, rows, cols), f32)
    edge_block = jax.ShapeDtypeStruct((held, 2, cols), f32)
    smem = pl.BlockSpec(memory_space=pltpu.SMEM)
    blocks, own, once, head, tail, *parts = pl.pallas_call(
        functools.partial(local_kernel, steps, peers, across),
        grid=(steps,),
        in_specs=[
            smem, whole(fields, species), by_rows(fields), whole(held, rows, cols), by_rows(species), by_rows(species),
            pl.BlockSpec((TILE, cols), lambda t: (t, 0)),
        ],
        out_specs=[
            whole(peers, lines, 1, LANES), whole(held, rows, cols), whole(held, rows, cols), whole(held, 2, cols), whole(held, 2, cols),
        ] + [whole(held, rows, cols)] * groups,
        out_shape=[jax.ShapeDtypeStruct((peers, lines, 1, LANES), f32), field_block, field_block, edge_block, edge_block] + [field_block] * groups,
        scratch_shapes=[
            pltpu.VMEM((flat_species, flat_fields), f32),
            pltpu.VMEM((flat_fields, flat_species), f32),
            pltpu.VMEM((flat_species, flat_fields), f32),
            pltpu.VMEM((fields, TILE, cols), f32),
        ],
        compiler_params=pltpu.CompilerParams(vmem_limit_bytes=32 * 2**20),
    )(place, loadings.T, latent, kappa_sq, coefs, counts, land)
    blocks = lax.all_to_all(blocks, ("gx", "gy"), 0, 0, tiled=True)
    arrived = [parts[0]]
    for distance in [2, 1, 3] if groups == 4 else range(1, groups):
        arrived.append(lax.ppermute(parts[distance], "sp", [(i, (i + distance) % groups) for i in range(groups)]))
    above = lax.ppermute(tail, "gx", [(i, i + 1) for i in range(down_count - 1)])
    below = lax.ppermute(head, "gx", [(i + 1, i) for i in range(down_count - 1)])
    vmem = pl.BlockSpec(memory_space=pltpu.VMEM)
    scale = 1.0 / math.sqrt(rows * down_count * cols * across)
    grad_latent, grad_loadings = pl.pallas_call(
        functools.partial(final_kernel, scale, down_count, across),
        in_specs=[smem] + [vmem] * (6 + groups),
        out_specs=[vmem, vmem],
        out_shape=[field_block, jax.ShapeDtypeStruct((fields, species), f32)],
        compiler_params=pltpu.CompilerParams(vmem_limit_bytes=32 * 2**20),
    )(place, blocks, own, once, kappa_sq, above, below, *arrived)
    return grad_latent, grad_loadings.T


def solution(mesh):
    return jax.shard_map(
        per_device,
        mesh=mesh,
        in_specs=(
            P(None, "gx", "gy"),
            P("sp", "gx", "gy"),
            P("sp", "gx", "gy"),
            P("sp", None),
            P("sp", "gx", "gy"),
            P("gx", "gy"),
        ),
        out_specs=(P("sp", "gx", "gy"), P("sp", None)),
        check_vma=False,
    )
```

time: 340 us -> 54.4 us (0.16)
  the two profiles are of different devices: /device:TPU:37 before, /device:TPU:216 now
where the time goes in v1:
time: 54.4 us; the launch traced here: 53.9 us
  starting transfers between devices  33.3 us (61%)
  waiting for transfers between devices  7.61 us (14%)
  Pallas kernels  6.35 us (12%)
  local copies, waits for them, and re-layouts  5.77 us (11%)
  between operations  0.73 us (1%)
    all_to_all x1, starting transfers between devices, per_device(): blocks = lax.all_to_all(blocks, ('gx', 'gy'), 0, 0, tiled=True)  14.8 us
    ppermute x3, starting transfers between devices, per_device(): lax.ppermute(parts[distance], 'sp', [(i, (i + distance) % groups) for i i...  12 us
    ppermute x1, waiting for transfers between devices, per_device(): lax.ppermute(head, 'gx', [(i + 1, i) for i in range(down_count - 1)])  7.6 us
    unnamed x14, local copies, waits for them, and re-layouts  5.77 us
    pallas_call x1, Pallas kernels, per_device(): pl.pallas_call(functools.partial(local_kernel, steps, peers, across), gri...  4.71 us
    ppermute x1, starting transfers between devices, per_device(): lax.ppermute(tail, 'gx', [(i, i + 1) for i in range(down_count - 1)])  4.61 us
    ppermute x1, starting transfers between devices, per_device(): lax.ppermute(head, 'gx', [(i + 1, i) for i in range(down_count - 1)])  1.92 us
    pallas_call x1, Pallas kernels, per_device(): pl.pallas_call(functools.partial(final_kernel, scale, down_count, across)...  1.64 us
  transfers between devices with their start and end apart: 6, of which 1 were waited for; matrix products, arithmetic and copies ran while one was open for 0% of the time, Pallas kernels for 0%

profile of v1, /device:TPU:216, one launch (start us, length us, event | category | flops | bytes accessed | tf_op | source)
XLA Modules:
  0.0 53.9 jit_solution(6652875426426140044)
XLA Ops:
  0.6 0.0 copy-start.6
  0.6 0.1 pad_add_fusion.place_ref
  0.7 0.6 %copy-done.6 = f32[32,16]{0,1:T(8,128)S(1)} copy-done((f32[32,16]{0,1:T(8,128)S(1)}, f32[32,16]{0,1:T(8,128)}, u32[]{:S(2)}) %copy-start.6) | copy-done | bytes 2072
  1.3 0.0 copy-start
  1.3 1.2 %copy-done = f32[32,16,512]{2,1,0:T(8,128)S(1)} copy-done((f32[32,16,512]{2,1,0:T(8,128)S(1)}, f32[32,16,512]{2,1,0:T(8,128)}, u32[]{:S(2)}) %copy-start) | copy-done | bytes 1048600
  2.6 0.0 copy-start.1
  2.6 1.2 %copy-done.1 = s32[32,16,512]{2,1,0:T(8,128)S(1)} copy-done((s32[32,16,512]{2,1,0:T(8,128)S(1)}, s32[32,16,512]{2,1,0:T(8,128)}, u32[]{:S(2)}) %copy-start.1) | copy-done | bytes 1048600
  3.8 0.0 copy-start.2
  3.8 0.9 %copy-done.2 = f32[4,16,512]{2,1,0:T(8,128)S(1)} copy-done((f32[4,16,512]{2,1,0:T(8,128)S(1)}, f32[4,16,512]{2,1,0:T(8,128)}, u32[]{:S(2)}) %copy-start.2) | copy-done | bytes 131096
  4.7 0.0 copy-start.4
  4.7 1.0 %copy-done.4 = f32[16,16,512]{2,1,0:T(8,128)S(1)} copy-done((f32[16,16,512]{2,1,0:T(8,128)S(1)}, f32[16,16,512]{2,1,0:T(8,128)}, u32[]{:S(2)}) %copy-start.4) | copy-done | bytes 524312
  5.7 0.0 copy-start.5
  5.7 0.8 %copy-done.5 = s32[16,512]{1,0:T(8,128)S(1)} copy-done((s32[16,512]{1,0:T(8,128)S(1)}, s32[16,512]{1,0:T(8,128)}, u32[]{:S(2)}) %copy-start.5) | copy-done | bytes 32792
  6.5 4.7 %shard_map.77 = (f32[128,5,1,128]{3,2,1,0:T(1,128)}, f32[4,16,512]{2,1,0:T(8,128)S(1)}, f32[4,16,512]{2,1,0:T(8,128)S(1)}, f32[4,2,512]{2,1,0:T(2,128)S(1)}, f32...) custom-call(s32[3]{0:T(128)S(1)} %pad_add_fusion.place_ref, ...), custom_call_target="tpu_custom_call" | custom-call | tf_op jit(solution)/shard_map/pallas_call | solution.py:201
  11.2 0.0 copy-start.3
  11.2 14.8 %all-to-all-start = ((f32[128,5,1,128]{3,2,1,0:T(1,128)}), f32[128,5,1,128]{3,2,1,0:T(1,128)S(1)}, u32[]{:S(2)}, u32[]{:S(2)}) async-start(f32[128,5,1,128]{3,2,1,0:T(1,128)} %get-tuple-element.13), calls=%async_computation | async-start | bytes 655360 | tf_op jit(solution)/shard_map/all_to_all | solution.py:220
  26.0 4.9 %collective-permute-start.2 = (f32[4,16,512]{2,1,0:T(8,128)S(1)}, f32[4,16,512]{2,1,0:T(8,128)S(1)}, u32[]{:S(2)}, u32[]{:S(2)}) collective-permute-start(f32[4,16,512]{2,1,0:T(8,128)S(1)} %get-tuple-element.19), channel_id=1, source_target_pairs={{0,2},{1,3},{2,0},{3,1},{4,6},{5,7},{6,4},{7,5},{8,10},{9,11},{10,... | collective-permute-start | bytes 393224 | tf_op jit(solution)/shard_map/ppermute | solution.py:223
  31.0 2.5 %collective-permute-start.3 = (f32[4,16,512]{2,1,0:T(8,128)S(1)}, f32[4,16,512]{2,1,0:T(8,128)S(1)}, u32[]{:S(2)}, u32[]{:S(2)}) collective-permute-start(f32[4,16,512]{2,1,0:T(8,128)S(1)} %get-tuple-element.20), channel_id=1, source_target_pairs={{0,1},{1,2},{2,3},{3,0},{4,5},{5,6},{6,7},{7,4},{8,9},{9,10},{10,1... | collective-permute-start | bytes 393224 | tf_op jit(solution)/shard_map/ppermute | solution.py:223
  33.5 4.6 %collective-permute-start.4 = (f32[4,16,512]{2,1,0:T(8,128)S(1)}, f32[4,16,512]{2,1,0:T(8,128)S(1)}, u32[]{:S(2)}, u32[]{:S(2)}) collective-permute-start(f32[4,16,512]{2,1,0:T(8,128)S(1)} %get-tuple-element.21), channel_id=1, source_target_pairs={{0,3},{1,0},{2,1},{3,2},{4,7},{5,4},{6,5},{7,6},{8,11},{9,8},{10,9... | collective-permute-start | bytes 393224 | tf_op jit(solution)/shard_map/ppermute | solution.py:223
  38.0 4.6 %collective-permute-start = (f32[4,2,512]{2,1,0:T(2,128)S(1)}, f32[4,2,512]{2,1,0:T(2,128)S(1)}, u32[]{:S(2)}, u32[]{:S(2)}) collective-permute-start(f32[4,2,512]{2,1,0:T(2,128)S(1)} %get-tuple-element.16), channel_id=1, source_target_pairs={{0,16},{16,32},{32,48},{48,64},{64,80},{80,96},{96,112},{112,128},... | collective-permute-start | bytes 49160 | tf_op jit(solution)/shard_map/ppermute | solution.py:224
  42.7 1.9 %collective-permute-start.1 = (f32[4,2,512]{2,1,0:T(2,128)S(1)}, f32[4,2,512]{2,1,0:T(2,128)S(1)}, u32[]{:S(2)}, u32[]{:S(2)}) collective-permute-start(f32[4,2,512]{2,1,0:T(2,128)S(1)} %get-tuple-element.17), channel_id=1, source_target_pairs={{16,0},{32,16},{48,32},{64,48},{80,64},{96,80},{112,96},{128,112},... | collective-permute-start | bytes 49160 | tf_op jit(solution)/shard_map/ppermute | solution.py:225
  44.6 0.0 collective-permute-done.above_ref
  44.6 7.6 %collective-permute-done.1.below_ref = f32[4,2,512]{2,1,0:T(2,128)S(1)} collective-permute-done((f32[4,2,512]{2,1,0:T(2,128)S(1)}, f32[4,2,512]{2,1,0:T(2,128)S(1)}, u32[]{:S(2)}, u32[]{:S(2)}) %collective-permute-start.1) | collective-permute-done | bytes 16416 | tf_op jit(solution)/shard_map/ppermute | solution.py:225
  52.2 0.0 collective-permute-done.2.rest_1_
  52.2 0.0 collective-permute-done.3.rest_2_
  52.2 0.0 collective-permute-done.4.rest_3_
  52.2 0.0 all-to-all-done.blocks_ref
  52.2 0.0 copy-done.3
  52.2 1.6 %shard_map.78 = (f32[4,16,512]{2,1,0:T(8,128)}, f32[16,32]{1,0:T(8,128)}) custom-call(s32[3]{0:T(128)S(1)} %pad_add_fusion.place_ref, f32[128,5,1,128]{3,2,1,0:T(1,128)S(1)} %all-to-all-done.blocks_ref, f32[4,16,512]{2,1,0:T(8,128)S(1)} %get-tuple-element.14.own_ref, f32[4,16,512]{2,1,0:T(8,128)S(1)} %get-tuple-element.15.once_ref, ...), custom_call_target="tpu_custom_call" | custom-call | tf_op jit(solution)/shard_map/pallas_call | solution.py:228
Async XLA Ops:
  0.6 0.7 %copy-start.6 = (f32[32,16]{0,1:T(8,128)S(1)}, f32[32,16]{0,1:T(8,128)}, u32[]{:S(2)}) copy-start(f32[32,16]{0,1:T(8,128)} %param.9) | copy-start | bytes 6148
  1.3 1.2 %copy-start = (f32[32,16,512]{2,1,0:T(8,128)S(1)}, f32[32,16,512]{2,1,0:T(8,128)}, u32[]{:S(2)}) copy-start(f32[32,16,512]{2,1,0:T(8,128)} %coefs_ref.1) | copy-start | bytes 3145732
  2.6 1.2 %copy-start.1 = (s32[32,16,512]{2,1,0:T(8,128)S(1)}, s32[32,16,512]{2,1,0:T(8,128)}, u32[]{:S(2)}) copy-start(s32[32,16,512]{2,1,0:T(8,128)} %counts_ref.1) | copy-start | bytes 3145732
  3.8 0.9 %copy-start.2 = (f32[4,16,512]{2,1,0:T(8,128)S(1)}, f32[4,16,512]{2,1,0:T(8,128)}, u32[]{:S(2)}) copy-start(f32[4,16,512]{2,1,0:T(8,128)} %kappa_ref.3) | copy-start | bytes 393220
  4.7 1.0 %copy-start.4 = (f32[16,16,512]{2,1,0:T(8,128)S(1)}, f32[16,16,512]{2,1,0:T(8,128)}, u32[]{:S(2)}) copy-start(f32[16,16,512]{2,1,0:T(8,128)} %latent_ref.1) | copy-start | bytes 1572868
  5.7 0.8 %copy-start.5 = (s32[16,512]{1,0:T(8,128)S(1)}, s32[16,512]{1,0:T(8,128)}, u32[]{:S(2)}) copy-start(s32[16,512]{1,0:T(8,128)} %land_ref.1) | copy-start | bytes 98308
  11.2 41.0 %copy-start.3 = (f32[4,16,512]{2,1,0:T(8,128)S(1)}, f32[4,16,512]{2,1,0:T(8,128)}, u32[]{:S(2)}) copy-start(f32[4,16,512]{2,1,0:T(8,128)} %kappa_ref.3) | copy-start | bytes 393220
  11.2 41.0 %all-to-all-start = ((f32[128,5,1,128]{3,2,1,0:T(1,128)}), f32[128,5,1,128]{3,2,1,0:T(1,128)S(1)}, u32[]{:S(2)}, u32[]{:S(2)}) async-start(f32[128,5,1,128]{3,2,1,0:T(1,128)} %get-tuple-element.13), calls=%async_computation | async-start | bytes 655360 | tf_op jit(solution)/shard_map/all_to_all | solution.py:220
  26.0 26.2 %collective-permute-start.2 = (f32[4,16,512]{2,1,0:T(8,128)S(1)}, f32[4,16,512]{2,1,0:T(8,128)S(1)}, u32[]{:S(2)}, u32[]{:S(2)}) collective-permute-start(f32[4,16,512]{2,1,0:T(8,128)S(1)} %get-tuple-element.19), channel_id=1, source_target_pairs={{0,2},{1,3},{2,0},{3,1},{4,6},{5,7},{6,4},{7,5},{8,10},{9,11},{10,... | collective-permute-start | bytes 393224 | tf_op jit(solution)/shard_map/ppermute | solution.py:223
  31.0 21.2 %collective-permute-start.3 = (f32[4,16,512]{2,1,0:T(8,128)S(1)}, f32[4,16,512]{2,1,0:T(8,128)S(1)}, u32[]{:S(2)}, u32[]{:S(2)}) collective-permute-start(f32[4,16,512]{2,1,0:T(8,128)S(1)} %get-tuple-element.20), channel_id=1, source_target_pairs={{0,1},{1,2},{2,3},{3,0},{4,5},{5,6},{6,7},{7,4},{8,9},{9,10},{10,1... | collective-permute-start | bytes 393224 | tf_op jit(solution)/shard_map/ppermute | solution.py:223
  33.5 18.7 %collective-permute-start.4 = (f32[4,16,512]{2,1,0:T(8,128)S(1)}, f32[4,16,512]{2,1,0:T(8,128)S(1)}, u32[]{:S(2)}, u32[]{:S(2)}) collective-permute-start(f32[4,16,512]{2,1,0:T(8,128)S(1)} %get-tuple-element.21), channel_id=1, source_target_pairs={{0,3},{1,0},{2,1},{3,2},{4,7},{5,4},{6,5},{7,6},{8,11},{9,8},{10,9... | collective-permute-start | bytes 393224 | tf_op jit(solution)/shard_map/ppermute | solution.py:223
  38.0 6.5 %collective-permute-start = (f32[4,2,512]{2,1,0:T(2,128)S(1)}, f32[4,2,512]{2,1,0:T(2,128)S(1)}, u32[]{:S(2)}, u32[]{:S(2)}) collective-permute-start(f32[4,2,512]{2,1,0:T(2,128)S(1)} %get-tuple-element.16), channel_id=1, source_target_pairs={{0,16},{16,32},{32,48},{48,64},{64,80},{80,96},{96,112},{112,128},... | collective-permute-start | bytes 49160 | tf_op jit(solution)/shard_map/ppermute | solution.py:224
  42.7 9.5 %collective-permute-start.1 = (f32[4,2,512]{2,1,0:T(2,128)S(1)}, f32[4,2,512]{2,1,0:T(2,128)S(1)}, u32[]{:S(2)}, u32[]{:S(2)}) collective-permute-start(f32[4,2,512]{2,1,0:T(2,128)S(1)} %get-tuple-element.17), channel_id=1, source_target_pairs={{16,0},{32,16},{48,32},{64,48},{80,64},{96,80},{112,96},{128,112},... | collective-permute-start | bytes 49160 | tf_op jit(solution)/shard_map/ppermute | solution.py:225

commit v2 on v1

v2 whole, which is shorter than its diff:
```python
import functools
import math

import jax
import jax.numpy as jnp
from jax import lax
from jax.experimental import pallas as pl
from jax.experimental.pallas import tpu as pltpu
from jax.sharding import PartitionSpec as P

HIGHEST = lax.Precision.HIGHEST
TILE = 8
LANES = 128
SPLIT = 1


def iota(shape, dim):
    return lax.broadcasted_iota(jnp.int32, shape, dim)


def dot(a, b, contract):
    return lax.dot_general(a, b, (contract, ((), ())), precision=HIGHEST, preferred_element_type=jnp.float32)


def operator(field, kappa, above, below, left, right):
    rows, cols = field.shape
    row, col = iota(field.shape, 0), iota(field.shape, 1)
    up = jnp.where(row == 0, above, pltpu.roll(field, 1, 0))
    down = jnp.where(row == rows - 1, below, pltpu.roll(field, rows - 1, 0))
    west = jnp.where(col == 0, left, pltpu.roll(field, 1, 1))
    east = jnp.where(col == cols - 1, right, pltpu.roll(field, cols - 1, 1))
    return (kappa + 4.0) * field - ((down + up) + (east + west))


def column_to_row(column, offset):
    shape = (column.shape[0], LANES)
    placed = jnp.where(iota(shape, 1) == iota(shape, 0) + offset, column, 0.0)
    return jnp.sum(placed, axis=0, keepdims=True)


def row_to_column(row, count, offset):
    shape = (count, LANES)
    placed = jnp.where(iota(shape, 1) == iota(shape, 0) + offset, row, 0.0)
    return jnp.sum(placed, axis=1, keepdims=True)


def parts_of(value, count):
    parts = []
    for _ in range(count):
        part = value.astype(jnp.bfloat16)
        parts.append(part)
        value = value - part.astype(jnp.float32)
    return parts


def spread_of(rows, cols, dim):
    one, many = iota((rows, cols), dim), iota((rows, cols), 1 - dim)
    return jnp.where(many // TILE == one, 1.0, 0.0)


def on_diagonal(value):
    return jnp.where(iota(value.shape, 0) % TILE == iota(value.shape, 1) % TILE, value, 0.0)


def bf16_dot(a, b, contract):
    return lax.dot_general(a, b, (contract, ((), ())), preferred_element_type=jnp.float32)


def local_kernel(
    peers, across,
    loadings_hbm, latent_hbm, kappa_hbm, coefs_hbm, counts_hbm, land_hbm,
    blocks_ref, own_ref, once_ref, head_ref, tail_ref, *rest,
):
    part_refs, scratch = rest[:-8], rest[-8:]
    (species_ref, loadings_ref, latent_ref, kappa_ref, coefs_ref, counts_ref, land_ref,
     sems) = scratch
    fields, species = loadings_ref.shape
    held, rows, cols = kappa_ref.shape
    sp, gy = lax.axis_index("sp"), lax.axis_index("gy")
    flat_fields, flat_species = fields * TILE, species * TILE
    width = cols // SPLIT
    pieces = [(r, c) for r in range(rows // TILE) for c in range(SPLIT)]
    copies = []
    for n, (r, c) in enumerate(pieces):
        at = (slice(None), pl.ds(r * TILE, TILE), pl.ds(c * width, width))
        pairs = [(latent_hbm, latent_ref), (coefs_hbm, coefs_ref), (counts_hbm, counts_ref)]
        copies.append([
            pltpu.make_async_copy(source.at[at], target.at[at], sems.at[3 * n + i])
            for i, (source, target) in enumerate(pairs)
        ])
    whole = 3 * len(pieces)
    loadings_copy = pltpu.make_async_copy(loadings_hbm, loadings_ref, sems.at[whole])
    land_copy = pltpu.make_async_copy(land_hbm, land_ref, sems.at[whole + 1])
    kappa_copy = pltpu.make_async_copy(kappa_hbm, kappa_ref, sems.at[whole + 2])
    latents = [piece[0] for piece in copies]
    others = [copy for piece in copies for copy in piece[1:]]
    for copy in [loadings_copy, *latents, kappa_copy, land_copy, *others]:
        copy.start()

    loadings_copy.wait()
    transposed = loadings_ref[...]
    wide = dot(transposed, spread_of(fields, flat_fields, 0), ((0,), (0,)))
    wide = jnp.broadcast_to(wide[:, None, :], (species, TILE, flat_fields)).reshape(flat_species, flat_fields)
    wide = parts_of(on_diagonal(wide), 3)
    wide = jnp.concatenate([wide[0], wide[0], wide[0], wide[1], wide[1], wide[2]], axis=1)
    tall = dot(transposed, spread_of(species, flat_species, 0), ((1,), (0,)))
    tall = jnp.broadcast_to(tall[:, None, :], (fields, TILE, flat_species)).reshape(flat_fields, flat_species)
    tall = parts_of(on_diagonal(tall), 2)
    tall = jnp.concatenate([tall[0], tall[0], tall[1]], axis=1)

    spans = [(slice(None), slice(r * TILE, (r + 1) * TILE), slice(c * width, (c + 1) * width)) for r, c in pieces]
    latents, mixes = [], []
    for n, at in enumerate(spans):
        copies[n][0].wait()
        latent = parts_of(latent_ref[at].reshape(flat_fields, width), 3)
        stacked = jnp.concatenate([latent[0], latent[1], latent[2], latent[0], latent[1], latent[0]], axis=0)
        mixes.append(bf16_dot(wide, stacked, ((1,), (0,))))
        latents.append(latent)
    land_copy.wait()
    gram = None
    for n, at in enumerate(spans):
        copies[n][1].wait()
        copies[n][2].wait()
        rate = jnp.exp(coefs_ref[at].reshape(flat_species, width) + mixes[n])
        counts = counts_ref[at].reshape(flat_species, width).astype(jnp.float32)
        land = jnp.broadcast_to(land_ref[at[1:]].astype(jnp.float32)[None], (species, TILE, width))
        resid = parts_of(land.reshape(flat_species, width) * (counts - rate), 2)
        latent = latents[n]
        stacked = jnp.concatenate([resid[0], resid[1], resid[0]], axis=0)
        species_ref[at] = bf16_dot(tall, stacked, ((1,), (0,))).reshape(fields, TILE, width)
        both = bf16_dot(resid[0], jnp.concatenate([latent[0], latent[1]], axis=0), ((1,), (1,)))
        partial = both[:, :flat_fields] + both[:, flat_fields:] + bf16_dot(resid[1], latent[0], ((1,), (1,)))
        gram = partial if gram is None else gram + partial

    kappa_copy.wait()
    first = sp * held
    own_ref[...] = latent_ref[pl.ds(first, held)]
    rim = rows * held
    west, east = jnp.zeros((1, LANES), jnp.float32), jnp.zeros((1, LANES), jnp.float32)
    for k in range(held):
        own = latent_ref[first + k]
        once = operator(own, kappa_ref[k], 0.0, 0.0, 0.0, 0.0)
        once_ref[k] = once
        head_ref[k] = jnp.concatenate([own[:1], once[:1]], axis=0)
        tail_ref[k] = jnp.concatenate([own[-1:], once[-1:]], axis=0)
        west = west + column_to_row(own[:, :1], k * rows) + column_to_row(once[:, :1], rim + k * rows)
        east = east + column_to_row(own[:, cols - 1:], k * rows) + column_to_row(once[:, cols - 1:], rim + k * rows)
    for distance, part_ref in enumerate(part_refs):
        owner = lax.rem(sp + distance, len(part_refs))
        part_ref[...] = species_ref[pl.ds(owner * held, held)]
    total = jnp.sum(on_diagonal(gram).reshape(species, TILE, flat_fields), axis=1)
    total = dot(spread_of(fields, flat_fields, 0), total, ((1,), (1,)))
    per_row = LANES // species
    sums = fields // per_row
    packed = jnp.concatenate([total[q * sums:(q + 1) * sums] for q in range(per_row)], axis=1)
    for peer in range(peers):
        blocks_ref[peer, :sums] = packed[:, None, :]
        blocks_ref[peer, sums] = jnp.where(peer % across < gy, west, east)


def final_kernel(
    scale, down_count, across,
    blocks_ref, own_ref, once_ref, kappa_ref, above_ref, below_ref, *rest,
):
    part_refs, (latent_ref, loadings_ref) = rest[:-2], rest[-2:]
    gy, gx = lax.axis_index("gy"), lax.axis_index("gx")
    held, rows, cols = own_ref.shape
    fields, species = loadings_ref.shape
    per_row = LANES // species
    sums = fields // per_row
    for r in range(sums):
        total = jnp.sum(blocks_ref[:, r, :, :], axis=0) * scale
        for q in range(per_row):
            loadings_ref[q * sums + r:q * sums + r + 1, :] = total[:, q * species:(q + 1) * species]

    rim = held * rows
    north, south = jnp.maximum(gx - 1, 0), jnp.minimum(gx + 1, down_count - 1)
    westward, eastward = jnp.maximum(gy - 1, 0), jnp.minimum(gy + 1, across - 1)
    has_north = jnp.where(gx > 0, 1.0, 0.0)
    has_south = jnp.where(gx < down_count - 1, 1.0, 0.0)
    has_west = jnp.where(gy > 0, 1.0, 0.0)
    has_east = jnp.where(gy < across - 1, 1.0, 0.0)

    def halo(i, j):
        return blocks_ref[i * across + j, sums]

    lane = iota((1, LANES), 1)

    def column(j, present):
        middle, upper, lower = halo(gx, j), halo(north, j) * has_north, halo(south, j) * has_south
        first = (lane >= rim) & (lane % rows == 0)
        last = (lane >= rim) & (lane % rows == rows - 1)
        middle = middle - jnp.where(first, pltpu.roll(upper, rim - (rows - 1), 1), 0.0)
        middle = middle - jnp.where(last, pltpu.roll(lower, rim + (rows - 1), 1), 0.0)
        middle = middle * present
        return row_to_column(middle, rim, 0), row_to_column(middle, rim, rim), upper * present, lower * present

    west, west_once, north_west, south_west = column(westward, has_west)
    east, east_once, north_east, south_east = column(eastward, has_east)
    for k in range(held):
        own, kappa = own_ref[k], kappa_ref[k]
        span = slice(k * rows, (k + 1) * rows)
        row, col = iota(own.shape, 0), iota(own.shape, 1)
        once = once_ref[k]
        once = once - jnp.where(row == 0, above_ref[k, :1], 0.0) - jnp.where(row == rows - 1, below_ref[k, :1], 0.0)
        once = once - jnp.where(col == 0, west[span], 0.0) - jnp.where(col == cols - 1, east[span], 0.0)
        edge = iota((1, cols), 1)

        def beside(sent, mine, left, right, at, present):
            corner = k * rows + at
            corners = jnp.where(edge == 0, left[:, corner:corner + 1], 0.0) + jnp.where(edge == cols - 1, right[:, corner:corner + 1], 0.0)
            return (sent - mine - corners) * present

        above = beside(above_ref[k, 1:], own[:1], north_west, north_east, rows - 1, has_north)
        below = beside(below_ref[k, 1:], own[rows - 1:], south_west, south_east, 0, has_south)
        left = (west_once[span] - own[:, :1]) * has_west
        right = (east_once[span] - own[:, cols - 1:]) * has_east
        prior = operator(once, kappa, above, below, left, right)
        species_sum = part_refs[0][k]
        for part_ref in part_refs[1:]:
            species_sum = species_sum + part_ref[k]
        latent_ref[k] = species_sum - prior


def per_device(latent, kappa_sq, coefs, loadings, counts, land):
    fields, rows, cols = latent.shape
    species = loadings.shape[0]
    held = kappa_sq.shape[0]
    down_count, across, groups = lax.axis_size("gx"), lax.axis_size("gy"), lax.axis_size("sp")
    peers = down_count * across
    lines = fields * species // LANES + 1
    f32 = jnp.float32
    field_block = jax.ShapeDtypeStruct((held, rows, cols), f32)
    edge_block = jax.ShapeDtypeStruct((held, 2, cols), f32)
    vmem = pl.BlockSpec(memory_space=pltpu.VMEM)
    hbm = pl.BlockSpec(memory_space=pltpu.HBM)
    pieces = rows // TILE * SPLIT
    blocks_shape = jax.ShapeDtypeStruct((peers, lines, 1, LANES), f32)
    blocks, own, once, head, tail, *parts = pl.pallas_call(
        functools.partial(local_kernel, peers, across),
        in_specs=[hbm] * 6,
        out_specs=[vmem] * (5 + groups),
        out_shape=[blocks_shape, field_block, field_block, edge_block, edge_block] + [field_block] * groups,
        scratch_shapes=[
            pltpu.VMEM(latent.shape, f32),
            pltpu.VMEM((fields, species), f32),
            pltpu.VMEM(latent.shape, f32),
            pltpu.VMEM(kappa_sq.shape, f32),
            pltpu.VMEM(coefs.shape, f32),
            pltpu.VMEM(counts.shape, jnp.int32),
            pltpu.VMEM(land.shape, jnp.int32),
            pltpu.SemaphoreType.DMA((3 * pieces + 3,)),
        ],
        compiler_params=pltpu.CompilerParams(vmem_limit_bytes=60 * 2**20),
    )(loadings.T, latent, kappa_sq, coefs, counts, land)
    blocks = lax.all_to_all(blocks, ("gx", "gy"), 0, 0, tiled=True)
    arrived = [parts[0]]
    for distance in [2, 1, 3] if groups == 4 else range(1, groups):
        arrived.append(lax.ppermute(parts[distance], "sp", [(i, (i + distance) % groups) for i in range(groups)]))
    above = lax.ppermute(tail, "gx", [(i, i + 1) for i in range(down_count - 1)])
    below = lax.ppermute(head, "gx", [(i + 1, i) for i in range(down_count - 1)])
    scale = 1.0 / math.sqrt(rows * down_count * cols * across)
    grad_latent, grad_loadings = pl.pallas_call(
        functools.partial(final_kernel, scale, down_count, across),
        in_specs=[vmem] * (6 + groups),
        out_specs=[vmem, vmem],
        out_shape=[field_block, jax.ShapeDtypeStruct((fields, species), f32)],
        compiler_params=pltpu.CompilerParams(vmem_limit_bytes=32 * 2**20),
    )(blocks, own, once, kappa_sq, above, below, *arrived)
    return grad_latent, grad_loadings.T


def solution(mesh):
    return jax.shard_map(
        per_device,
        mesh=mesh,
        in_specs=(
            P(None, "gx", "gy"),
            P("sp", "gx", "gy"),
            P("sp", "gx", "gy"),
            P("sp", None),
            P("sp", "gx", "gy"),
            P("gx", "gy"),
        ),
        out_specs=(P("sp", "gx", "gy"), P("sp", None)),
        check_vma=False,
    )
```

time: 54.4 us -> 47.5 us (0.87)
  local copies, waits for them, and re-layouts: 5.77 us -> 0.03 us
  Pallas kernels: 6.35 us -> 5.21 us
    unnamed x14 -> x10, local copies, waits for them, and re-layouts: 5.77 us -> 0.03 us
    pallas_call x1, Pallas kernels: 4.71 us -> 4.11 us  [per_device(): pl.pallas_call(functools.partial(local_kernel, peers, across), in_specs=[...]
where the time goes in v2:
time: 47.5 us; the launch traced here: 47.2 us
  starting transfers between devices  33.4 us (70%)
  waiting for transfers between devices  7.82 us (16%)
  Pallas kernels  5.21 us (11%)
  between operations  0.79 us (2%)
    all_to_all x1, starting transfers between devices, per_device(): blocks = lax.all_to_all(blocks, ('gx', 'gy'), 0, 0, tiled=True)  14.8 us
    ppermute x3, starting transfers between devices, per_device(): lax.ppermute(parts[distance], 'sp', [(i, (i + distance) % groups) for i i...  12 us
    ppermute x1, waiting for transfers between devices, per_device(): lax.ppermute(head, 'gx', [(i + 1, i) for i in range(down_count - 1)])  7.81 us
    ppermute x1, starting transfers between devices, per_device(): lax.ppermute(tail, 'gx', [(i, i + 1) for i in range(down_count - 1)])  4.61 us
    pallas_call x1, Pallas kernels, per_device(): pl.pallas_call(functools.partial(local_kernel, peers, across), in_specs=[...  4.11 us
    ppermute x1, starting transfers between devices, per_device(): lax.ppermute(head, 'gx', [(i + 1, i) for i in range(down_count - 1)])  1.92 us
    pallas_call x1, Pallas kernels, per_device(): pl.pallas_call(functools.partial(final_kernel, scale, down_count, across)...  1.1 us
  transfers between devices with their start and end apart: 6, of which 1 were waited for; matrix products, arithmetic and copies ran while one was open for 0% of the time, Pallas kernels for 0%

profile of v2, /device:TPU:216, one launch (start us, length us, event | category | flops | bytes accessed | tf_op | source)
XLA Modules:
  0.0 47.2 jit_solution(12191326091257560723)
XLA Ops:
  0.6 4.1 %shard_map.77 = (f32[128,5,1,128]{3,2,1,0:T(1,128)}, f32[4,16,512]{2,1,0:T(8,128)}, f32[4,16,512]{2,1,0:T(8,128)}, f32[4,2,512]{2,1,0:T(2,128)}, f32[4,2,512]{2,...) custom-call(f32[16,32]{1,0:T(8,128)} %bitcast.2, ...), custom_call_target="tpu_custom_call" | custom-call | tf_op jit(solution)/shard_map/pallas_call | solution.py:239
  4.8 0.0 copy-start.4
  4.8 0.0 copy-start
  4.8 0.0 copy-start.1
  4.8 0.0 copy-start.2
  4.8 0.0 copy-start.3
  4.8 14.8 %all-to-all-start = ((f32[128,5,1,128]{3,2,1,0:T(1,128)}), f32[128,5,1,128]{3,2,1,0:T(1,128)S(1)}, u32[]{:S(2)}, u32[]{:S(2)}) async-start(f32[128,5,1,128]{3,2,1,0:T(1,128)} %get-tuple-element.13), calls=%async_computation | async-start | bytes 655360 | tf_op jit(solution)/shard_map/all_to_all | solution.py:256
  19.7 4.9 %collective-permute-start.2 = (f32[4,16,512]{2,1,0:T(8,128)}, f32[4,16,512]{2,1,0:T(8,128)S(1)}, u32[]{:S(2)}, u32[]{:S(2)}) collective-permute-start(f32[4,16,512]{2,1,0:T(8,128)} %get-tuple-element.19), channel_id=1, source_target_pairs={{0,2},{1,3},{2,0},{3,1},{4,6},{5,7},{6,4},{7,5},{8,10},{9,11},{10,... | collective-permute-start | bytes 393224 | tf_op jit(solution)/shard_map/ppermute | solution.py:259
  24.6 2.5 %collective-permute-start.3 = (f32[4,16,512]{2,1,0:T(8,128)}, f32[4,16,512]{2,1,0:T(8,128)S(1)}, u32[]{:S(2)}, u32[]{:S(2)}) collective-permute-start(f32[4,16,512]{2,1,0:T(8,128)} %get-tuple-element.20), channel_id=1, source_target_pairs={{0,1},{1,2},{2,3},{3,0},{4,5},{5,6},{6,7},{7,4},{8,9},{9,10},{10,1... | collective-permute-start | bytes 393224 | tf_op jit(solution)/shard_map/ppermute | solution.py:259
  27.1 0.0 copy-done.4
  27.1 4.5 %collective-permute-start.4 = (f32[4,16,512]{2,1,0:T(8,128)S(1)}, f32[4,16,512]{2,1,0:T(8,128)S(1)}, u32[]{:S(2)}, u32[]{:S(2)}) collective-permute-start(f32[4,16,512]{2,1,0:T(8,128)S(1)} %copy-done.4), channel_id=1, source_target_pairs={{0,3},{1,0},{2,1},{3,2},{4,7},{5,4},{6,5},{7,6},{8,11},{9,8},{10,9... | collective-permute-start | bytes 393224 | tf_op jit(solution)/shard_map/ppermute | solution.py:259
  31.7 4.6 %collective-permute-start = (f32[4,2,512]{2,1,0:T(2,128)}, f32[4,2,512]{2,1,0:T(2,128)S(1)}, u32[]{:S(2)}, u32[]{:S(2)}) collective-permute-start(f32[4,2,512]{2,1,0:T(2,128)} %get-tuple-element.16), channel_id=1, source_target_pairs={{0,16},{16,32},{32,48},{48,64},{64,80},{80,96},{96,112},{112,128},... | collective-permute-start | bytes 49160 | tf_op jit(solution)/shard_map/ppermute | solution.py:260
  36.3 1.9 %collective-permute-start.1 = (f32[4,2,512]{2,1,0:T(2,128)}, f32[4,2,512]{2,1,0:T(2,128)S(1)}, u32[]{:S(2)}, u32[]{:S(2)}) collective-permute-start(f32[4,2,512]{2,1,0:T(2,128)} %get-tuple-element.17), channel_id=1, source_target_pairs={{16,0},{32,16},{48,32},{64,48},{80,64},{96,80},{112,96},{128,112},... | collective-permute-start | bytes 49160 | tf_op jit(solution)/shard_map/ppermute | solution.py:261
  38.2 0.0 collective-permute-done.above_ref
  38.2 7.8 %collective-permute-done.1.below_ref = f32[4,2,512]{2,1,0:T(2,128)S(1)} collective-permute-done((f32[4,2,512]{2,1,0:T(2,128)}, f32[4,2,512]{2,1,0:T(2,128)S(1)}, u32[]{:S(2)}, u32[]{:S(2)}) %collective-permute-start.1) | collective-permute-done | bytes 16416 | tf_op jit(solution)/shard_map/ppermute | solution.py:261
  46.0 0.0 collective-permute-done.2.rest_1_
  46.0 0.0 collective-permute-done.3.rest_2_
  46.0 0.0 collective-permute-done.4.rest_3_
  46.0 0.0 all-to-all-done.blocks_ref
  46.1 0.0 copy-done
  46.1 0.0 copy-done.1
  46.1 0.0 copy-done.2
  46.1 0.0 copy-done.3
  46.1 1.1 %shard_map.78 = (f32[4,16,512]{2,1,0:T(8,128)}, f32[16,32]{1,0:T(8,128)}) custom-call(f32[128,5,1,128]{3,2,1,0:T(1,128)S(1)} %all-to-all-done.blocks_ref, f32[4,16,512]{2,1,0:T(8,128)S(1)} %copy-done.1, f32[4,16,512]{2,1,0:T(8,128)S(1)} %copy-done.2, f32[4,16,512]{2,1,0:T(8,128)S(1)} %copy-done, f32[4,2,512]{2,1,0:T(2,128)S(1)} %collective-permute-done.above_ref, ...), custom_call_target="tpu_custom_call" | custom-call | tf_op jit(solution)/shard_map/pallas_call | solution.py:263
Async XLA Ops:
  4.8 22.4 %copy-start.4 = (f32[4,16,512]{2,1,0:T(8,128)S(1)}, f32[4,16,512]{2,1,0:T(8,128)}, u32[]{:S(2)}) copy-start(f32[4,16,512]{2,1,0:T(8,128)} %get-tuple-element.21) | copy-start | bytes 393220
  4.8 41.3 %copy-start = (f32[4,16,512]{2,1,0:T(8,128)S(1)}, f32[4,16,512]{2,1,0:T(8,128)}, u32[]{:S(2)}) copy-start(f32[4,16,512]{2,1,0:T(8,128)} %kappa_ref.1) | copy-start | bytes 393220
  4.8 41.3 %copy-start.1 = (f32[4,16,512]{2,1,0:T(8,128)S(1)}, f32[4,16,512]{2,1,0:T(8,128)}, u32[]{:S(2)}) copy-start(f32[4,16,512]{2,1,0:T(8,128)} %get-tuple-element.14.own_ref) | copy-start | bytes 393220
  4.8 41.3 %copy-start.2 = (f32[4,16,512]{2,1,0:T(8,128)S(1)}, f32[4,16,512]{2,1,0:T(8,128)}, u32[]{:S(2)}) copy-start(f32[4,16,512]{2,1,0:T(8,128)} %get-tuple-element.15.once_ref) | copy-start | bytes 393220
  4.8 41.3 %copy-start.3 = (f32[4,16,512]{2,1,0:T(8,128)S(1)}, f32[4,16,512]{2,1,0:T(8,128)}, u32[]{:S(2)}) copy-start(f32[4,16,512]{2,1,0:T(8,128)} %get-tuple-element.18.rest_0_) | copy-start | bytes 393220
  4.8 41.2 %all-to-all-start = ((f32[128,5,1,128]{3,2,1,0:T(1,128)}), f32[128,5,1,128]{3,2,1,0:T(1,128)S(1)}, u32[]{:S(2)}, u32[]{:S(2)}) async-start(f32[128,5,1,128]{3,2,1,0:T(1,128)} %get-tuple-element.13), calls=%async_computation | async-start | bytes 655360 | tf_op jit(solution)/shard_map/all_to_all | solution.py:256
  19.7 26.4 %collective-permute-start.2 = (f32[4,16,512]{2,1,0:T(8,128)}, f32[4,16,512]{2,1,0:T(8,128)S(1)}, u32[]{:S(2)}, u32[]{:S(2)}) collective-permute-start(f32[4,16,512]{2,1,0:T(8,128)} %get-tuple-element.19), channel_id=1, source_target_pairs={{0,2},{1,3},{2,0},{3,1},{4,6},{5,7},{6,4},{7,5},{8,10},{9,11},{10,... | collective-permute-start | bytes 393224 | tf_op jit(solution)/shard_map/ppermute | solution.py:259
  24.6 21.5 %collective-permute-start.3 = (f32[4,16,512]{2,1,0:T(8,128)}, f32[4,16,512]{2,1,0:T(8,128)S(1)}, u32[]{:S(2)}, u32[]{:S(2)}) collective-permute-start(f32[4,16,512]{2,1,0:T(8,128)} %get-tuple-element.20), channel_id=1, source_target_pairs={{0,1},{1,2},{2,3},{3,0},{4,5},{5,6},{6,7},{7,4},{8,9},{9,10},{10,1... | collective-permute-start | bytes 393224 | tf_op jit(solution)/shard_map/ppermute | solution.py:259
  27.1 18.9 %collective-permute-start.4 = (f32[4,16,512]{2,1,0:T(8,128)S(1)}, f32[4,16,512]{2,1,0:T(8,128)S(1)}, u32[]{:S(2)}, u32[]{:S(2)}) collective-permute-start(f32[4,16,512]{2,1,0:T(8,128)S(1)} %copy-done.4), channel_id=1, source_target_pairs={{0,3},{1,0},{2,1},{3,2},{4,7},{5,4},{6,5},{7,6},{8,11},{9,8},{10,9... | collective-permute-start | bytes 393224 | tf_op jit(solution)/shard_map/ppermute | solution.py:259
  31.7 6.5 %collective-permute-start = (f32[4,2,512]{2,1,0:T(2,128)}, f32[4,2,512]{2,1,0:T(2,128)S(1)}, u32[]{:S(2)}, u32[]{:S(2)}) collective-permute-start(f32[4,2,512]{2,1,0:T(2,128)} %get-tuple-element.16), channel_id=1, source_target_pairs={{0,16},{16,32},{32,48},{48,64},{64,80},{80,96},{96,112},{112,128},... | collective-permute-start | bytes 49160 | tf_op jit(solution)/shard_map/ppermute | solution.py:260
  36.3 9.8 %collective-permute-start.1 = (f32[4,2,512]{2,1,0:T(2,128)}, f32[4,2,512]{2,1,0:T(2,128)S(1)}, u32[]{:S(2)}, u32[]{:S(2)}) collective-permute-start(f32[4,2,512]{2,1,0:T(2,128)} %get-tuple-element.17), channel_id=1, source_target_pairs={{16,0},{32,16},{48,32},{64,48},{80,64},{96,80},{112,96},{128,112},... | collective-permute-start | bytes 49160 | tf_op jit(solution)/shard_map/ppermute | solution.py:261

commit v3 on v2

--- a/solution.py
+++ b/solution.py
@@ -44,6 +44,10 @@
     return jnp.sum(placed, axis=1, keepdims=True)
 
 
+def partner(place, distance, count):
+    return place ^ distance if count & (count - 1) == 0 else (place + distance) % count
+
+
 def parts_of(value, count):
     parts = []
     for _ in range(count):
@@ -69,7 +73,7 @@
 def local_kernel(
     peers, across,
     loadings_hbm, latent_hbm, kappa_hbm, coefs_hbm, counts_hbm, land_hbm,
-    blocks_ref, own_ref, once_ref, head_ref, tail_ref, *rest,
+    blocks_ref, own_ref, once_ref, odd_ref, even_ref, *rest,
 ):
     part_refs, scratch = rest[:-8], rest[-8:]
     (species_ref, loadings_ref, latent_ref, kappa_ref, coefs_ref, counts_ref, land_ref,
@@ -134,6 +138,7 @@
 
     kappa_copy.wait()
     first = sp * held
+    is_even = lax.axis_index("gx") % 2 == 0
     own_ref[...] = latent_ref[pl.ds(first, held)]
     rim = rows * held
     west, east = jnp.zeros((1, LANES), jnp.float32), jnp.zeros((1, LANES), jnp.float32)
@@ -141,12 +146,14 @@
         own = latent_ref[first + k]
         once = operator(own, kappa_ref[k], 0.0, 0.0, 0.0, 0.0)
         once_ref[k] = once
-        head_ref[k] = jnp.concatenate([own[:1], once[:1]], axis=0)
-        tail_ref[k] = jnp.concatenate([own[-1:], once[-1:]], axis=0)
+        head = jnp.concatenate([own[:1], once[:1]], axis=0)
+        tail = jnp.concatenate([own[-1:], once[-1:]], axis=0)
+        odd_ref[k] = jnp.where(is_even, head, tail)
+        even_ref[k] = jnp.where(is_even, tail, head)
         west = west + column_to_row(own[:, :1], k * rows) + column_to_row(once[:, :1], rim + k * rows)
         east = east + column_to_row(own[:, cols - 1:], k * rows) + column_to_row(once[:, cols - 1:], rim + k * rows)
     for distance, part_ref in enumerate(part_refs):
-        owner = lax.rem(sp + distance, len(part_refs))
+        owner = partner(sp, distance, len(part_refs))
         part_ref[...] = species_ref[pl.ds(owner * held, held)]
     total = jnp.sum(on_diagonal(gram).reshape(species, TILE, flat_fields), axis=1)
     total = dot(spread_of(fields, flat_fields, 0), total, ((1,), (1,)))
@@ -160,7 +167,7 @@
 
 def final_kernel(
     scale, down_count, across,
-    blocks_ref, own_ref, once_ref, kappa_ref, above_ref, below_ref, *rest,
+    blocks_ref, own_ref, once_ref, kappa_ref, odd_ref, even_ref, *rest,
 ):
     part_refs, (latent_ref, loadings_ref) = rest[:-2], rest[-2:]
     gy, gx = lax.axis_index("gy"), lax.axis_index("gx")
@@ -174,6 +181,7 @@
             loadings_ref[q * sums + r:q * sums + r + 1, :] = total[:, q * species:(q + 1) * species]
 
     rim = held * rows
+    is_even = gx % 2 == 0
     north, south = jnp.maximum(gx - 1, 0), jnp.minimum(gx + 1, down_count - 1)
     westward, eastward = jnp.maximum(gy - 1, 0), jnp.minimum(gy + 1, across - 1)
     has_north = jnp.where(gx > 0, 1.0, 0.0)
@@ -199,10 +207,12 @@
     east, east_once, north_east, south_east = column(eastward, has_east)
     for k in range(held):
         own, kappa = own_ref[k], kappa_ref[k]
+        above_edge = jnp.where(is_even, odd_ref[k], even_ref[k])
+        below_edge = jnp.where(is_even, even_ref[k], odd_ref[k])
         span = slice(k * rows, (k + 1) * rows)
         row, col = iota(own.shape, 0), iota(own.shape, 1)
         once = once_ref[k]
-        once = once - jnp.where(row == 0, above_ref[k, :1], 0.0) - jnp.where(row == rows - 1, below_ref[k, :1], 0.0)
+        once = once - jnp.where(row == 0, above_edge[:1], 0.0) - jnp.where(row == rows - 1, below_edge[:1], 0.0)
         once = once - jnp.where(col == 0, west[span], 0.0) - jnp.where(col == cols - 1, east[span], 0.0)
         edge = iota((1, cols), 1)
 
@@ -211,8 +221,8 @@
             corners = jnp.where(edge == 0, left[:, corner:corner + 1], 0.0) + jnp.where(edge == cols - 1, right[:, corner:corner + 1], 0.0)
             return (sent - mine - corners) * present
 
-        above = beside(above_ref[k, 1:], own[:1], north_west, north_east, rows - 1, has_north)
-        below = beside(below_ref[k, 1:], own[rows - 1:], south_west, south_east, 0, has_south)
+        above = beside(above_edge[1:], own[:1], north_west, north_east, rows - 1, has_north)
+        below = beside(below_edge[1:], own[rows - 1:], south_west, south_east, 0, has_south)
         left = (west_once[span] - own[:, :1]) * has_west
         right = (east_once[span] - own[:, cols - 1:]) * has_east
         prior = operator(once, kappa, above, below, left, right)
@@ -236,7 +246,7 @@
     hbm = pl.BlockSpec(memory_space=pltpu.HBM)
     pieces = rows // TILE * SPLIT
     blocks_shape = jax.ShapeDtypeStruct((peers, lines, 1, LANES), f32)
-    blocks, own, once, head, tail, *parts = pl.pallas_call(
+    blocks, own, once, odd_edge, even_edge, *parts = pl.pallas_call(
         functools.partial(local_kernel, peers, across),
         in_specs=[hbm] * 6,
         out_specs=[vmem] * (5 + groups),
@@ -256,9 +266,13 @@
     blocks = lax.all_to_all(blocks, ("gx", "gy"), 0, 0, tiled=True)
     arrived = [parts[0]]
     for distance in [2, 1, 3] if groups == 4 else range(1, groups):
-        arrived.append(lax.ppermute(parts[distance], "sp", [(i, (i + distance) % groups) for i in range(groups)]))
-    above = lax.ppermute(tail, "gx", [(i, i + 1) for i in range(down_count - 1)])
-    below = lax.ppermute(head, "gx", [(i + 1, i) for i in range(down_count - 1)])
+        arrived.append(lax.ppermute(parts[distance], "sp", [(i, partner(i, distance, groups)) for i in range(groups)]))
+
+    def exchanged(edge, first):
+        pairs = [(i, i + 1) for i in range(first, down_count - 1, 2)]
+        return lax.ppermute(edge, "gx", pairs + [(j, i) for i, j in pairs])
+
+    by_odd, by_even = exchanged(odd_edge, 1), exchanged(even_edge, 0)
     scale = 1.0 / math.sqrt(rows * down_count * cols * across)
     grad_latent, grad_loadings = pl.pallas_call(
         functools.partial(final_kernel, scale, down_count, across),
@@ -266,7 +280,7 @@
         out_specs=[vmem, vmem],
         out_shape=[field_block, jax.ShapeDtypeStruct((fields, species), f32)],
         compiler_params=pltpu.CompilerParams(vmem_limit_bytes=32 * 2**20),
-    )(blocks, own, once, kappa_sq, above, below, *arrived)
+    )(blocks, own, once, kappa_sq, by_odd, by_even, *arrived)
     return grad_latent, grad_loadings.T
 
 

time: 47.5 us -> 45.6 us (0.960)
  the two profiles are of different devices: /device:TPU:216 before, /device:TPU:40 now
where the time goes in v3:
time: 45.6 us; the launch traced here: 45.3 us
  starting transfers between devices  35.3 us (77%)
  Pallas kernels  5.22 us (11%)
  waiting for transfers between devices  3.92 us (9%)
  between operations  0.78 us (2%)
    all_to_all x1, starting transfers between devices, per_device(): blocks = lax.all_to_all(blocks, ('gx', 'gy'), 0, 0, tiled=True)  17.5 us
    ppermute x3, starting transfers between devices, per_device(): lax.ppermute(parts[distance], 'sp', [(i, partner(i, distance, groups)) fo...  9.9 us
    ppermute x2, starting transfers between devices, exchanged(): return lax.ppermute(edge, 'gx', pairs + [(j, i) for i, j in pairs])  7.96 us
    pallas_call x1, Pallas kernels, per_device(): pl.pallas_call(functools.partial(local_kernel, peers, across), in_specs=[...  4.11 us
    ppermute x2, waiting for transfers between devices, exchanged(): return lax.ppermute(edge, 'gx', pairs + [(j, i) for i, j in pairs])  3.91 us
    pallas_call x1, Pallas kernels, per_device(): pl.pallas_call(functools.partial(final_kernel, scale, down_count, across)...  1.11 us
  transfers between devices with their start and end apart: 6, of which 2 were waited for; matrix products, arithmetic and copies ran while one was open for 0% of the time, Pallas kernels for 0%

profile of v3, /device:TPU:40, one launch (start us, length us, event | category | flops | bytes accessed | tf_op | source)
XLA Modules:
  0.0 45.3 jit_solution(13112007112225852637)
XLA Ops:
  0.6 4.1 %shard_map.77 = (f32[128,5,1,128]{3,2,1,0:T(1,128)}, f32[4,16,512]{2,1,0:T(8,128)}, f32[4,16,512]{2,1,0:T(8,128)}, f32[4,2,512]{2,1,0:T(2,128)}, f32[4,2,512]{2,...) custom-call(f32[16,32]{1,0:T(8,128)} %bitcast.2, ...), custom_call_target="tpu_custom_call" | custom-call | tf_op jit(solution)/shard_map/pallas_call | solution.py:249
  4.7 0.0 copy-start.4
  4.8 0.0 copy-start
  4.8 0.0 copy-start.1
  4.8 0.0 copy-start.2
  4.8 0.0 copy-start.3
  4.8 17.5 %all-to-all-start = ((f32[128,5,1,128]{3,2,1,0:T(1,128)}), f32[128,5,1,128]{3,2,1,0:T(1,128)S(1)}, u32[]{:S(2)}, u32[]{:S(2)}) async-start(f32[128,5,1,128]{3,2,1,0:T(1,128)} %get-tuple-element.13), calls=%async_computation | async-start | bytes 655360 | tf_op jit(solution)/shard_map/all_to_all | solution.py:266
  22.3 4.9 %collective-permute-start.2 = (f32[4,16,512]{2,1,0:T(8,128)}, f32[4,16,512]{2,1,0:T(8,128)S(1)}, u32[]{:S(2)}, u32[]{:S(2)}) collective-permute-start(f32[4,16,512]{2,1,0:T(8,128)} %get-tuple-element.19), channel_id=1, source_target_pairs={{0,2},{1,3},{2,0},{3,1},{4,6},{5,7},{6,4},{7,5},{8,10},{9,11},{10,... | collective-permute-start | bytes 393224 | tf_op jit(solution)/shard_map/ppermute | solution.py:269
  27.2 2.5 %collective-permute-start.3 = (f32[4,16,512]{2,1,0:T(8,128)}, f32[4,16,512]{2,1,0:T(8,128)S(1)}, u32[]{:S(2)}, u32[]{:S(2)}) collective-permute-start(f32[4,16,512]{2,1,0:T(8,128)} %get-tuple-element.20), channel_id=1, source_target_pairs={{0,1},{1,0},{2,3},{3,2},{4,5},{5,4},{6,7},{7,6},{8,9},{9,8},{10,11... | collective-permute-start | bytes 393224 | tf_op jit(solution)/shard_map/ppermute | solution.py:269
  29.7 0.0 copy-done.4
  29.7 2.5 %collective-permute-start.4 = (f32[4,16,512]{2,1,0:T(8,128)S(1)}, f32[4,16,512]{2,1,0:T(8,128)S(1)}, u32[]{:S(2)}, u32[]{:S(2)}) collective-permute-start(f32[4,16,512]{2,1,0:T(8,128)S(1)} %copy-done.4), channel_id=1, source_target_pairs={{0,3},{1,2},{2,1},{3,0},{4,7},{5,6},{6,5},{7,4},{8,11},{9,10},{10,... | collective-permute-start | bytes 393224 | tf_op jit(solution)/shard_map/ppermute | solution.py:269
  32.2 6.0 %collective-permute-start = (f32[4,2,512]{2,1,0:T(2,128)}, f32[4,2,512]{2,1,0:T(2,128)S(1)}, u32[]{:S(2)}, u32[]{:S(2)}) collective-permute-start(f32[4,2,512]{2,1,0:T(2,128)} %get-tuple-element.16), channel_id=1, source_target_pairs={{16,32},{48,64},{80,96},{112,128},{144,160},{176,192},{208,224},{2... | collective-permute-start | bytes 49160 | tf_op jit(solution)/shard_map/ppermute | solution.py:273
  38.3 1.9 %collective-permute-start.1 = (f32[4,2,512]{2,1,0:T(2,128)}, f32[4,2,512]{2,1,0:T(2,128)S(1)}, u32[]{:S(2)}, u32[]{:S(2)}) collective-permute-start(f32[4,2,512]{2,1,0:T(2,128)} %get-tuple-element.17), channel_id=1, source_target_pairs={{0,16},{32,48},{64,80},{96,112},{128,144},{160,176},{192,208},{224... | collective-permute-start | bytes 49160 | tf_op jit(solution)/shard_map/ppermute | solution.py:273
  40.2 0.7 %collective-permute-done.odd_ref = f32[4,2,512]{2,1,0:T(2,128)S(1)} collective-permute-done((f32[4,2,512]{2,1,0:T(2,128)}, f32[4,2,512]{2,1,0:T(2,128)S(1)}, u32[]{:S(2)}, u32[]{:S(2)}) %collective-permute-start) | collective-permute-done | bytes 16416 | tf_op jit(solution)/shard_map/ppermute | solution.py:273
  40.9 3.2 %collective-permute-done.1.even_ref = f32[4,2,512]{2,1,0:T(2,128)S(1)} collective-permute-done((f32[4,2,512]{2,1,0:T(2,128)}, f32[4,2,512]{2,1,0:T(2,128)S(1)}, u32[]{:S(2)}, u32[]{:S(2)}) %collective-permute-start.1) | collective-permute-done | bytes 16416 | tf_op jit(solution)/shard_map/ppermute | solution.py:273
  44.1 0.0 collective-permute-done.2.rest_1_
  44.1 0.0 collective-permute-done.3.rest_2_
  44.1 0.0 collective-permute-done.4.rest_3_
  44.1 0.0 all-to-all-done.blocks_ref
  44.1 0.0 copy-done
  44.2 0.0 copy-done.1
  44.2 0.0 copy-done.2
  44.2 0.0 copy-done.3
  44.2 1.1 %shard_map.78 = (f32[4,16,512]{2,1,0:T(8,128)}, f32[16,32]{1,0:T(8,128)}) custom-call(f32[128,5,1,128]{3,2,1,0:T(1,128)S(1)} %all-to-all-done.blocks_ref, f32[4,16,512]{2,1,0:T(8,128)S(1)} %copy-done.1, f32[4,16,512]{2,1,0:T(8,128)S(1)} %copy-done.2, f32[4,16,512]{2,1,0:T(8,128)S(1)} %copy-done, f32[4,2,512]{2,1,0:T(2,128)S(1)} %collective-permute-done.odd_ref, ...), custom_call_target="tpu_custom_call" | custom-call | tf_op jit(solution)/shard_map/pallas_call | solution.py:277
Async XLA Ops:
  4.7 25.0 %copy-start.4 = (f32[4,16,512]{2,1,0:T(8,128)S(1)}, f32[4,16,512]{2,1,0:T(8,128)}, u32[]{:S(2)}) copy-start(f32[4,16,512]{2,1,0:T(8,128)} %get-tuple-element.21) | copy-start | bytes 393220
  4.8 39.4 %copy-start = (f32[4,16,512]{2,1,0:T(8,128)S(1)}, f32[4,16,512]{2,1,0:T(8,128)}, u32[]{:S(2)}) copy-start(f32[4,16,512]{2,1,0:T(8,128)} %kappa_ref.1) | copy-start | bytes 393220
  4.8 39.4 %copy-start.1 = (f32[4,16,512]{2,1,0:T(8,128)S(1)}, f32[4,16,512]{2,1,0:T(8,128)}, u32[]{:S(2)}) copy-start(f32[4,16,512]{2,1,0:T(8,128)} %get-tuple-element.14.own_ref) | copy-start | bytes 393220
  4.8 39.4 %copy-start.2 = (f32[4,16,512]{2,1,0:T(8,128)S(1)}, f32[4,16,512]{2,1,0:T(8,128)}, u32[]{:S(2)}) copy-start(f32[4,16,512]{2,1,0:T(8,128)} %get-tuple-element.15.once_ref) | copy-start | bytes 393220
  4.8 39.4 %copy-start.3 = (f32[4,16,512]{2,1,0:T(8,128)S(1)}, f32[4,16,512]{2,1,0:T(8,128)}, u32[]{:S(2)}) copy-start(f32[4,16,512]{2,1,0:T(8,128)} %get-tuple-element.18.rest_0_) | copy-start | bytes 393220
  4.8 39.3 %all-to-all-start = ((f32[128,5,1,128]{3,2,1,0:T(1,128)}), f32[128,5,1,128]{3,2,1,0:T(1,128)S(1)}, u32[]{:S(2)}, u32[]{:S(2)}) async-start(f32[128,5,1,128]{3,2,1,0:T(1,128)} %get-tuple-element.13), calls=%async_computation | async-start | bytes 655360 | tf_op jit(solution)/shard_map/all_to_all | solution.py:266
  22.3 21.8 %collective-permute-start.2 = (f32[4,16,512]{2,1,0:T(8,128)}, f32[4,16,512]{2,1,0:T(8,128)S(1)}, u32[]{:S(2)}, u32[]{:S(2)}) collective-permute-start(f32[4,16,512]{2,1,0:T(8,128)} %get-tuple-element.19), channel_id=1, source_target_pairs={{0,2},{1,3},{2,0},{3,1},{4,6},{5,7},{6,4},{7,5},{8,10},{9,11},{10,... | collective-permute-start | bytes 393224 | tf_op jit(solution)/shard_map/ppermute | solution.py:269
  27.2 16.9 %collective-permute-start.3 = (f32[4,16,512]{2,1,0:T(8,128)}, f32[4,16,512]{2,1,0:T(8,128)S(1)}, u32[]{:S(2)}, u32[]{:S(2)}) collective-permute-start(f32[4,16,512]{2,1,0:T(8,128)} %get-tuple-element.20), channel_id=1, source_target_pairs={{0,1},{1,0},{2,3},{3,2},{4,5},{5,4},{6,7},{7,6},{8,9},{9,8},{10,11... | collective-permute-start | bytes 393224 | tf_op jit(solution)/shard_map/ppermute | solution.py:269
  29.7 14.4 %collective-permute-start.4 = (f32[4,16,512]{2,1,0:T(8,128)S(1)}, f32[4,16,512]{2,1,0:T(8,128)S(1)}, u32[]{:S(2)}, u32[]{:S(2)}) collective-permute-start(f32[4,16,512]{2,1,0:T(8,128)S(1)} %copy-done.4), channel_id=1, source_target_pairs={{0,3},{1,2},{2,1},{3,0},{4,7},{5,6},{6,5},{7,4},{8,11},{9,10},{10,... | collective-permute-start | bytes 393224 | tf_op jit(solution)/shard_map/ppermute | solution.py:269
  32.2 8.6 %collective-permute-start = (f32[4,2,512]{2,1,0:T(2,128)}, f32[4,2,512]{2,1,0:T(2,128)S(1)}, u32[]{:S(2)}, u32[]{:S(2)}) collective-permute-start(f32[4,2,512]{2,1,0:T(2,128)} %get-tuple-element.16), channel_id=1, source_target_pairs={{16,32},{48,64},{80,96},{112,128},{144,160},{176,192},{208,224},{2... | collective-permute-start | bytes 49160 | tf_op jit(solution)/shard_map/ppermute | solution.py:273
  38.3 5.8 %collective-permute-start.1 = (f32[4,2,512]{2,1,0:T(2,128)}, f32[4,2,512]{2,1,0:T(2,128)S(1)}, u32[]{:S(2)}, u32[]{:S(2)}) collective-permute-start(f32[4,2,512]{2,1,0:T(2,128)} %get-tuple-element.17), channel_id=1, source_target_pairs={{0,16},{32,48},{64,80},{96,112},{128,144},{160,176},{192,208},{224... | collective-permute-start | bytes 49160 | tf_op jit(solution)/shard_map/ppermute | solution.py:273

commit v4 on v3

--- a/solution.py
+++ b/solution.py
@@ -12,6 +12,7 @@
 TILE = 8
 LANES = 128
 SPLIT = 1
+NEAR, FAR = 1, 3
 
 
 def iota(shape, dim):
@@ -44,10 +45,6 @@
     return jnp.sum(placed, axis=1, keepdims=True)
 
 
-def partner(place, distance, count):
-    return place ^ distance if count & (count - 1) == 0 else (place + distance) % count
-
-
 def parts_of(value, count):
     parts = []
     for _ in range(count):
@@ -73,11 +70,9 @@
 def local_kernel(
     peers, across,
     loadings_hbm, latent_hbm, kappa_hbm, coefs_hbm, counts_hbm, land_hbm,
-    blocks_ref, own_ref, once_ref, odd_ref, even_ref, *rest,
+    blocks_ref, own_ref, odd_ref, even_ref, sent_ref, kept_ref,
+    species_ref, loadings_ref, latent_ref, kappa_ref, coefs_ref, counts_ref, land_ref, sems,
 ):
-    part_refs, scratch = rest[:-8], rest[-8:]
-    (species_ref, loadings_ref, latent_ref, kappa_ref, coefs_ref, counts_ref, land_ref,
-     sems) = scratch
     fields, species = loadings_ref.shape
     held, rows, cols = kappa_ref.shape
     sp, gy = lax.axis_index("sp"), lax.axis_index("gy")
@@ -145,16 +140,15 @@
     for k in range(held):
         own = latent_ref[first + k]
         once = operator(own, kappa_ref[k], 0.0, 0.0, 0.0, 0.0)
-        once_ref[k] = once
         head = jnp.concatenate([own[:1], once[:1]], axis=0)
         tail = jnp.concatenate([own[-1:], once[-1:]], axis=0)
         odd_ref[k] = jnp.where(is_even, head, tail)
         even_ref[k] = jnp.where(is_even, tail, head)
         west = west + column_to_row(own[:, :1], k * rows) + column_to_row(once[:, :1], rim + k * rows)
         east = east + column_to_row(own[:, cols - 1:], k * rows) + column_to_row(once[:, cols - 1:], rim + k * rows)
-    for distance, part_ref in enumerate(part_refs):
-        owner = partner(sp, distance, len(part_refs))
-        part_ref[...] = species_ref[pl.ds(owner * held, held)]
+    for ref, owners in ((kept_ref, (sp, sp ^ FAR)), (sent_ref, (sp ^ NEAR, sp ^ NEAR ^ FAR))):
+        for half, owner in enumerate(owners):
+            ref[half] = species_ref[pl.ds(owner * held, held)]
     total = jnp.sum(on_diagonal(gram).reshape(species, TILE, flat_fields), axis=1)
     total = dot(spread_of(fields, flat_fields, 0), total, ((1,), (1,)))
     per_row = LANES // species
@@ -165,11 +159,28 @@
         blocks_ref[peer, sums] = jnp.where(peer % across < gy, west, east)
 
 
-def final_kernel(
-    scale, down_count, across,
-    blocks_ref, own_ref, once_ref, kappa_ref, odd_ref, even_ref, *rest,
-):
-    part_refs, (latent_ref, loadings_ref) = rest[:-2], rest[-2:]
+def add_kernel(kept_ref, received_ref, mine_ref, sent_ref):
+    mine_ref[...] = kept_ref[0] + received_ref[0]
+    sent_ref[...] = kept_ref[1] + received_ref[1]
+
+
+def prior_kernel(down_count, own_ref, kappa_ref, odd_ref, even_ref, prior_ref):
+    gx = lax.axis_index("gx")
+    held, rows, cols = own_ref.shape
+    is_even = gx % 2 == 0
+    has_north = jnp.where(gx > 0, 1.0, 0.0)
+    has_south = jnp.where(gx < down_count - 1, 1.0, 0.0)
+    for k in range(held):
+        own, kappa = own_ref[k], kappa_ref[k]
+        above_edge = jnp.where(is_even, odd_ref[k], even_ref[k])
+        below_edge = jnp.where(is_even, even_ref[k], odd_ref[k])
+        once = operator(own, kappa, above_edge[:1], below_edge[:1], 0.0, 0.0)
+        above = (above_edge[1:] - own[:1]) * has_north
+        below = (below_edge[1:] - own[rows - 1:]) * has_south
+        prior_ref[k] = operator(once, kappa, above, below, 0.0, 0.0)
+
+
+def final_kernel(scale, down_count, across, blocks_ref, own_ref, kappa_ref, prior_ref, mine_ref, other_ref, latent_ref, loadings_ref):
     gy, gx = lax.axis_index("gy"), lax.axis_index("gx")
     held, rows, cols = own_ref.shape
     fields, species = loadings_ref.shape
@@ -181,55 +192,40 @@
             loadings_ref[q * sums + r:q * sums + r + 1, :] = total[:, q * species:(q + 1) * species]
 
     rim = held * rows
-    is_even = gx % 2 == 0
     north, south = jnp.maximum(gx - 1, 0), jnp.minimum(gx + 1, down_count - 1)
-    westward, eastward = jnp.maximum(gy - 1, 0), jnp.minimum(gy + 1, across - 1)
     has_north = jnp.where(gx > 0, 1.0, 0.0)
     has_south = jnp.where(gx < down_count - 1, 1.0, 0.0)
-    has_west = jnp.where(gy > 0, 1.0, 0.0)
-    has_east = jnp.where(gy < across - 1, 1.0, 0.0)
-
-    def halo(i, j):
-        return blocks_ref[i * across + j, sums]
-
     lane = iota((1, LANES), 1)
 
     def column(j, present):
-        middle, upper, lower = halo(gx, j), halo(north, j) * has_north, halo(south, j) * has_south
-        first = (lane >= rim) & (lane % rows == 0)
-        last = (lane >= rim) & (lane % rows == rows - 1)
-        middle = middle - jnp.where(first, pltpu.roll(upper, rim - (rows - 1), 1), 0.0)
-        middle = middle - jnp.where(last, pltpu.roll(lower, rim + (rows - 1), 1), 0.0)
-        middle = middle * present
-        return row_to_column(middle, rim, 0), row_to_column(middle, rim, rim), upper * present, lower * present
-
-    west, west_once, north_west, south_west = column(westward, has_west)
-    east, east_once, north_east, south_east = column(eastward, has_east)
+        middle, upper, lower = blocks_ref[gx * across + j, sums], blocks_ref[north * across + j, sums], blocks_ref[south * across + j, sums]
+        first, last = lane % rows == 0, lane % rows == rows - 1
+        corners = jnp.where(first, pltpu.roll(upper, LANES - (rows - 1), 1), 0.0) * has_north
+        corners = corners + jnp.where(last, pltpu.roll(lower, rows - 1, 1), 0.0) * has_south
+        corners = jnp.where(lane < rim, corners, 0.0)
+        once = pltpu.roll(middle, LANES - rim, 1) - corners
+        return [row_to_column(row * present, rim, 0) for row in (middle, once, corners)]
+
+    west = column(jnp.maximum(gy - 1, 0), jnp.where(gy > 0, 1.0, 0.0))
+    east = column(jnp.minimum(gy + 1, across - 1), jnp.where(gy < across - 1, 1.0, 0.0))
+    row, col = iota((rows, LANES), 0), iota((rows, LANES), 1)
+
+    def addition(k, columns, at, own, kappa, edge, inner, present):
+        field, once, corners = [value[k * rows:(k + 1) * rows] for value in columns]
+        once = once - own * present
+        field = jnp.broadcast_to(field, (rows, LANES))
+        beside = jnp.where(row == 0, 0.0, pltpu.roll(field, 1, 0)) + jnp.where(row == rows - 1, 0.0, pltpu.roll(field, rows - 1, 0))
+        outer = beside - (kappa + 4.0) * field - once + corners
+        return jnp.where(col == edge, outer, 0.0) + jnp.where(col == inner, field, 0.0)
+
     for k in range(held):
-        own, kappa = own_ref[k], kappa_ref[k]
-        above_edge = jnp.where(is_even, odd_ref[k], even_ref[k])
-        below_edge = jnp.where(is_even, even_ref[k], odd_ref[k])
-        span = slice(k * rows, (k + 1) * rows)
-        row, col = iota(own.shape, 0), iota(own.shape, 1)
-        once = once_ref[k]
-        once = once - jnp.where(row == 0, above_edge[:1], 0.0) - jnp.where(row == rows - 1, below_edge[:1], 0.0)
-        once = once - jnp.where(col == 0, west[span], 0.0) - jnp.where(col == cols - 1, east[span], 0.0)
-        edge = iota((1, cols), 1)
-
-        def beside(sent, mine, left, right, at, present):
-            corner = k * rows + at
-            corners = jnp.where(edge == 0, left[:, corner:corner + 1], 0.0) + jnp.where(edge == cols - 1, right[:, corner:corner + 1], 0.0)
-            return (sent - mine - corners) * present
-
-        above = beside(above_edge[1:], own[:1], north_west, north_east, rows - 1, has_north)
-        below = beside(below_edge[1:], own[rows - 1:], south_west, south_east, 0, has_south)
-        left = (west_once[span] - own[:, :1]) * has_west
-        right = (east_once[span] - own[:, cols - 1:]) * has_east
-        prior = operator(once, kappa, above, below, left, right)
-        species_sum = part_refs[0][k]
-        for part_ref in part_refs[1:]:
-            species_sum = species_sum + part_ref[k]
-        latent_ref[k] = species_sum - prior
+        latent_ref[k] = mine_ref[k] + other_ref[k] - prior_ref[k]
+        span = slice(0, LANES)
+        latent_ref[k, :, span] -= addition(
+            k, west, span, own_ref[k, :, :1], kappa_ref[k, :, span], 0, 1, jnp.where(gy > 0, 1.0, 0.0))
+        span = slice(cols - LANES, cols)
+        latent_ref[k, :, span] -= addition(
+            k, east, span, own_ref[k, :, cols - 1:], kappa_ref[k, :, span], LANES - 1, LANES - 2, jnp.where(gy < across - 1, 1.0, 0.0))
 
 
 def per_device(latent, kappa_sq, coefs, loadings, counts, land):
@@ -245,12 +241,14 @@
     vmem = pl.BlockSpec(memory_space=pltpu.VMEM)
     hbm = pl.BlockSpec(memory_space=pltpu.HBM)
     pieces = rows // TILE * SPLIT
-    blocks_shape = jax.ShapeDtypeStruct((peers, lines, 1, LANES), f32)
-    blocks, own, once, odd_edge, even_edge, *parts = pl.pallas_call(
+    half_block = jax.ShapeDtypeStruct((groups // 2, held, rows, cols), f32)
+    blocks, own, odd_edge, even_edge, sent, kept = pl.pallas_call(
         functools.partial(local_kernel, peers, across),
         in_specs=[hbm] * 6,
-        out_specs=[vmem] * (5 + groups),
-        out_shape=[blocks_shape, field_block, field_block, edge_block, edge_block] + [field_block] * groups,
+        out_specs=[vmem] * 6,
+        out_shape=[
+            jax.ShapeDtypeStruct((peers, lines, 1, LANES), f32), field_block, edge_block, edge_block, half_block, half_block,
+        ],
         scratch_shapes=[
             pltpu.VMEM(latent.shape, f32),
             pltpu.VMEM((fields, species), f32),
@@ -264,23 +262,39 @@
         compiler_params=pltpu.CompilerParams(vmem_limit_bytes=60 * 2**20),
     )(loadings.T, latent, kappa_sq, coefs, counts, land)
     blocks = lax.all_to_all(blocks, ("gx", "gy"), 0, 0, tiled=True)
-    arrived = [parts[0]]
-    for distance in [2, 1, 3] if groups == 4 else range(1, groups):
-        arrived.append(lax.ppermute(parts[distance], "sp", [(i, partner(i, distance, groups)) for i in range(groups)]))
 
     def exchanged(edge, first):
         pairs = [(i, i + 1) for i in range(first, down_count - 1, 2)]
         return lax.ppermute(edge, "gx", pairs + [(j, i) for i, j in pairs])
 
     by_odd, by_even = exchanged(odd_edge, 1), exchanged(even_edge, 0)
+    params = pltpu.CompilerParams(vmem_limit_bytes=16 * 2**20)
+    received = lax.ppermute(sent, "sp", [(i, i ^ NEAR) for i in range(groups)])
+    mine, sent = pl.pallas_call(
+        add_kernel,
+        in_specs=[vmem] * 2,
+        out_specs=[vmem] * 2,
+        out_shape=[field_block] * 2,
+        compiler_params=params,
+        cost_estimate=pl.CostEstimate(flops=10**6, bytes_accessed=2**20, transcendentals=0),
+    )(kept, received)
+    other = lax.ppermute(sent, "sp", [(i, i ^ FAR) for i in range(groups)])
+    prior = pl.pallas_call(
+        functools.partial(prior_kernel, down_count),
+        in_specs=[vmem] * 4,
+        out_specs=vmem,
+        out_shape=field_block,
+        compiler_params=params,
+        cost_estimate=pl.CostEstimate(flops=3*10**9, bytes_accessed=2**20, transcendentals=0),
+    )(own, kappa_sq, by_odd, by_even)
     scale = 1.0 / math.sqrt(rows * down_count * cols * across)
     grad_latent, grad_loadings = pl.pallas_call(
         functools.partial(final_kernel, scale, down_count, across),
-        in_specs=[vmem] * (6 + groups),
+        in_specs=[vmem] * 6,
         out_specs=[vmem, vmem],
         out_shape=[field_block, jax.ShapeDtypeStruct((fields, species), f32)],
-        compiler_params=pltpu.CompilerParams(vmem_limit_bytes=32 * 2**20),
-    )(blocks, own, once, kappa_sq, by_odd, by_even, *arrived)
+        compiler_params=params,
+    )(blocks, own, kappa_sq, prior, mine, other)
     return grad_latent, grad_loadings.T
 
 

time: 45.6 us -> 43.3 us (0.950)
  starting transfers between devices: 35.3 us -> 33 us
    ppermute x2, waiting for transfers between devices: 3.91 us -> 0.01 us  [exchanged(): return lax.ppermute(edge, 'gx', pairs + [(j, i) for i, j in pairs])]
    ppermute x3 -> x2, waiting for transfers between devices: 0.01 us -> 3.74 us  [the longest x1 3.73 us: per_device(): other = lax.ppermute(sent, 'sp', [(i, i ^ FAR) for i in range(groups)])]
    ppermute x3 -> x2, starting transfers between devices: 9.9 us -> 7.54 us  [the longest x1 4.14 us: per_device(): other = lax.ppermute(sent, 'sp', [(i, i ^ FAR) for i in range(groups)])]
  transfers between devices with their start and end apart: 6 -> 5, of which waited for: 2 -> 1; matrix products, arithmetic and copies ran while one was open for 0% -> 0% of each run, Pallas kernels for 0% -> 1%
where the time goes in v4:
time: 43.3 us; the launch traced here: 43 us
  starting transfers between devices  33 us (76%)
  Pallas kernels  5.42 us (13%)
  waiting for transfers between devices  3.74 us (9%)
  between operations  0.81 us (2%)
    all_to_all x1, starting transfers between devices, per_device(): blocks = lax.all_to_all(blocks, ('gx', 'gy'), 0, 0, tiled=True)  17.5 us
    ppermute x2, starting transfers between devices, exchanged(): return lax.ppermute(edge, 'gx', pairs + [(j, i) for i, j in pairs])  7.96 us
    ppermute x1, starting transfers between devices, per_device(): other = lax.ppermute(sent, 'sp', [(i, i ^ FAR) for i in range(groups)])  4.14 us
    pallas_call x1, Pallas kernels, per_device(): pl.pallas_call(functools.partial(local_kernel, peers, across), in_specs=[...  4.07 us
    ppermute x1, waiting for transfers between devices, per_device(): other = lax.ppermute(sent, 'sp', [(i, i ^ FAR) for i in range(groups)])  3.73 us
    ppermute x1, starting transfers between devices, per_device(): received = lax.ppermute(sent, 'sp', [(i, i ^ NEAR) for i in range(groups)])  3.4 us
    pallas_call x1, Pallas kernels, per_device(): pl.pallas_call(functools.partial(final_kernel, scale, down_count, across)...  1.03 us
  transfers between devices with their start and end apart: 5, of which 1 were waited for; matrix products, arithmetic and copies ran while one was open for 0% of the time, Pallas kernels for 1%

profile of v4, /device:TPU:40, one launch (start us, length us, event | category | flops | bytes accessed | tf_op | source)
XLA Modules:
  0.0 43.0 jit_solution(14713635795456224784)
XLA Ops:
  0.6 4.1 %shard_map.77 = (f32[128,5,1,128]{3,2,1,0:T(1,128)}, f32[4,16,512]{2,1,0:T(8,128)}, f32[4,2,512]{2,1,0:T(2,128)}, f32[4,2,512]{2,1,0:T(2,128)}, f32[2,4,16,512]{3,2,1,0:T(8,128)}, /*index=5*/f32[2,4,16,512]{3,2,1,0:T(8,128)}) custom-call(f32[16,32]{1,0:T(8,128)} %bitcast.2, f32[16,16,512]{2,1,0:T(8,128)} %latent_hbm.1, f32[4,16,512]{2,1,0:T(8,128)} %kappa_ref.3, ...), custom_call_target="tpu_custom_call" | custom-call | tf_op jit(solution)/shard_map/pallas_call | solution.py:245
  4.7 0.0 copy-start.3
  4.7 0.0 copy-start.5
  4.7 0.0 copy-start.4
  4.7 0.0 copy-start.1
  4.7 17.5 %all-to-all-start = ((f32[128,5,1,128]{3,2,1,0:T(1,128)}), f32[128,5,1,128]{3,2,1,0:T(1,128)S(1)}, u32[]{:S(2)}, u32[]{:S(2)}) async-start(f32[128,5,1,128]{3,2,1,0:T(1,128)} %get-tuple-element.12), calls=%async_computation | async-start | bytes 655360 | tf_op jit(solution)/shard_map/all_to_all | solution.py:264
  22.2 0.0 copy-done.3
  22.2 3.4 %collective-permute-start.2 = (f32[2,4,16,512]{3,2,1,0:T(8,128)S(1)}, f32[2,4,16,512]{3,2,1,0:T(8,128)S(1)}, u32[]{:S(2)}, u32[]{:S(2)}) collective-permute-start(f32[2,4,16,512]{3,2,1,0:T(8,128)S(1)} %copy-done.3), channel_id=1, source_target_pairs={{0,1},{1,0},{2,3},{3,2},{4,5},{5,4},{6,7},{7,6},{8,9},{9,8},{10,11... | collective-permute-start | bytes 786440 | tf_op jit(solution)/shard_map/ppermute | solution.py:272
  25.6 0.0 copy-done.5
  25.7 6.0 %collective-permute-start = (f32[4,2,512]{2,1,0:T(2,128)S(1)}, f32[4,2,512]{2,1,0:T(2,128)S(1)}, u32[]{:S(2)}, u32[]{:S(2)}) collective-permute-start(f32[4,2,512]{2,1,0:T(2,128)S(1)} %copy-done.5), channel_id=1, source_target_pairs={{16,32},{48,64},{80,96},{112,128},{144,160},{176,192},{208,224},{2... | collective-permute-start | bytes 49160 | tf_op jit(solution)/shard_map/ppermute | solution.py:268
  31.7 0.0 copy-done.4
  31.7 1.9 %collective-permute-start.1 = (f32[4,2,512]{2,1,0:T(2,128)S(1)}, f32[4,2,512]{2,1,0:T(2,128)S(1)}, u32[]{:S(2)}, u32[]{:S(2)}) collective-permute-start(f32[4,2,512]{2,1,0:T(2,128)S(1)} %copy-done.4), channel_id=1, source_target_pairs={{0,16},{32,48},{64,80},{96,112},{128,144},{160,176},{192,208},{224... | collective-permute-start | bytes 49160 | tf_op jit(solution)/shard_map/ppermute | solution.py:268
  33.6 0.0 collective-permute-done.2.received_ref
  33.7 0.0 copy-done.1
  33.7 0.0 copy-start
  33.7 0.0 copy-start.2
  33.7 4.1 %collective-permute-start.3 = (f32[4,16,512]{2,1,0:T(8,128)S(1)}, f32[4,16,512]{2,1,0:T(8,128)S(1)}, u32[]{:S(2)}, u32[]{:S(2)}) collective-permute-start(f32[4,16,512]{2,1,0:T(8,128)S(1)} %get-tuple-element.19), channel_id=1, source_target_pairs={{0,3},{1,2},{2,1},{3,0},{4,7},{5,6},{6,5},{7,4},{8,11},{9,10},{10,... | collective-permute-start | bytes 393224 | tf_op jit(solution)/shard_map/ppermute | solution.py:281
  37.9 0.0 collective-permute-done.odd_ref
  37.9 0.0 collective-permute-done.1.even_ref
  37.9 0.0 copy-done
  37.9 0.0 copy-done.2
  37.9 0.3 shard_map.78.prior_ref
  38.2 3.7 %collective-permute-done.3.other_ref = f32[4,16,512]{2,1,0:T(8,128)S(1)} collective-permute-done((f32[4,16,512]{2,1,0:T(8,128)S(1)}, f32[4,16,512]{2,1,0:T(8,128)S(1)}, u32[]{:S(2)}, u32[]{:S(2)}) %collective-permute-start.3) | collective-permute-done | bytes 131104 | tf_op jit(solution)/shard_map/ppermute | solution.py:281
  42.0 0.0 all-to-all-done.blocks_ref
  42.0 1.0 %shard_map.80 = (f32[4,16,512]{2,1,0:T(8,128)}, f32[16,32]{1,0:T(8,128)}) custom-call(f32[128,5,1,128]{3,2,1,0:T(1,128)S(1)} %all-to-all-done.blocks_ref, f32[4,16,512]{2,1,0:T(8,128)S(1)} %copy-done.2, f32[4,16,512]{2,1,0:T(8,128)S(1)} %copy-done, f32[4,16,512]{2,1,0:T(8,128)S(1)} %shard_map.78.prior_ref, f32[4,16,512]{2,1,0:T(8,128)S(1)} %get-tuple-element.18.mine_ref, ...), custom_call_target="tpu_custom_call" | custom-call | tf_op jit(solution)/shard_map/pallas_call | solution.py:291
  (1 shorter events, 0.0 us)
Async XLA Ops:
  4.7 17.5 %copy-start.3 = (f32[2,4,16,512]{3,2,1,0:T(8,128)S(1)}, f32[2,4,16,512]{3,2,1,0:T(8,128)}, u32[]{:S(2)}) copy-start(f32[2,4,16,512]{3,2,1,0:T(8,128)} %get-tuple-element.17) | copy-start | bytes 786436
  4.7 20.9 %copy-start.5 = (f32[4,2,512]{2,1,0:T(2,128)S(1)}, f32[4,2,512]{2,1,0:T(2,128)}, u32[]{:S(2)}) copy-start(f32[4,2,512]{2,1,0:T(2,128)} %get-tuple-element.14) | copy-start | bytes 49156
  4.7 27.0 %copy-start.4 = (f32[4,2,512]{2,1,0:T(2,128)S(1)}, f32[4,2,512]{2,1,0:T(2,128)}, u32[]{:S(2)}) copy-start(f32[4,2,512]{2,1,0:T(2,128)} %get-tuple-element.15) | copy-start | bytes 49156
  4.7 28.9 %copy-start.1 = (f32[2,4,16,512]{3,2,1,0:T(8,128)S(1)}, f32[2,4,16,512]{3,2,1,0:T(8,128)}, u32[]{:S(2)}) copy-start(f32[2,4,16,512]{3,2,1,0:T(8,128)} %get-tuple-element.16.kept_ref) | copy-start | bytes 786436
  4.7 37.2 %all-to-all-start = ((f32[128,5,1,128]{3,2,1,0:T(1,128)}), f32[128,5,1,128]{3,2,1,0:T(1,128)S(1)}, u32[]{:S(2)}, u32[]{:S(2)}) async-start(f32[128,5,1,128]{3,2,1,0:T(1,128)} %get-tuple-element.12), calls=%async_computation | async-start | bytes 655360 | tf_op jit(solution)/shard_map/all_to_all | solution.py:264
  22.2 11.4 %collective-permute-start.2 = (f32[2,4,16,512]{3,2,1,0:T(8,128)S(1)}, f32[2,4,16,512]{3,2,1,0:T(8,128)S(1)}, u32[]{:S(2)}, u32[]{:S(2)}) collective-permute-start(f32[2,4,16,512]{3,2,1,0:T(8,128)S(1)} %copy-done.3), channel_id=1, source_target_pairs={{0,1},{1,0},{2,3},{3,2},{4,5},{5,4},{6,7},{7,6},{8,9},{9,8},{10,11... | collective-permute-start | bytes 786440 | tf_op jit(solution)/shard_map/ppermute | solution.py:272
  25.7 12.2 %collective-permute-start = (f32[4,2,512]{2,1,0:T(2,128)S(1)}, f32[4,2,512]{2,1,0:T(2,128)S(1)}, u32[]{:S(2)}, u32[]{:S(2)}) collective-permute-start(f32[4,2,512]{2,1,0:T(2,128)S(1)} %copy-done.5), channel_id=1, source_target_pairs={{16,32},{48,64},{80,96},{112,128},{144,160},{176,192},{208,224},{2... | collective-permute-start | bytes 49160 | tf_op jit(solution)/shard_map/ppermute | solution.py:268
  31.7 6.2 %collective-permute-start.1 = (f32[4,2,512]{2,1,0:T(2,128)S(1)}, f32[4,2,512]{2,1,0:T(2,128)S(1)}, u32[]{:S(2)}, u32[]{:S(2)}) collective-permute-start(f32[4,2,512]{2,1,0:T(2,128)S(1)} %copy-done.4), channel_id=1, source_target_pairs={{0,16},{32,48},{64,80},{96,112},{128,144},{160,176},{192,208},{224... | collective-permute-start | bytes 49160 | tf_op jit(solution)/shard_map/ppermute | solution.py:268
  33.7 4.2 %copy-start = (f32[4,16,512]{2,1,0:T(8,128)S(1)}, f32[4,16,512]{2,1,0:T(8,128)}, u32[]{:S(2)}) copy-start(f32[4,16,512]{2,1,0:T(8,128)} %kappa_ref.3) | copy-start | bytes 393220
  33.7 4.2 %copy-start.2 = (f32[4,16,512]{2,1,0:T(8,128)S(1)}, f32[4,16,512]{2,1,0:T(8,128)}, u32[]{:S(2)}) copy-start(f32[4,16,512]{2,1,0:T(8,128)} %get-tuple-element.13.own_ref) | copy-start | bytes 393220
  33.7 8.2 %collective-permute-start.3 = (f32[4,16,512]{2,1,0:T(8,128)S(1)}, f32[4,16,512]{2,1,0:T(8,128)S(1)}, u32[]{:S(2)}, u32[]{:S(2)}) collective-permute-start(f32[4,16,512]{2,1,0:T(8,128)S(1)} %get-tuple-element.19), channel_id=1, source_target_pairs={{0,3},{1,2},{2,1},{3,0},{4,7},{5,6},{6,5},{7,4},{8,11},{9,10},{10,... | collective-permute-start | bytes 393224 | tf_op jit(solution)/shard_map/ppermute | solution.py:281

commit v5 on v4

--- a/solution.py
+++ b/solution.py
@@ -125,11 +125,11 @@
         land = jnp.broadcast_to(land_ref[at[1:]].astype(jnp.float32)[None], (species, TILE, width))
         resid = parts_of(land.reshape(flat_species, width) * (counts - rate), 2)
         latent = latents[n]
-        stacked = jnp.concatenate([resid[0], resid[1], resid[0]], axis=0)
-        species_ref[at] = bf16_dot(tall, stacked, ((1,), (0,))).reshape(fields, TILE, width)
         both = bf16_dot(resid[0], jnp.concatenate([latent[0], latent[1]], axis=0), ((1,), (1,)))
         partial = both[:, :flat_fields] + both[:, flat_fields:] + bf16_dot(resid[1], latent[0], ((1,), (1,)))
         gram = partial if gram is None else gram + partial
+        stacked = jnp.concatenate([resid[0], resid[1], resid[0]], axis=0)
+        species_ref[at] = bf16_dot(tall, stacked, ((1,), (0,))).reshape(fields, TILE, width)
 
     kappa_copy.wait()
     first = sp * held
@@ -164,24 +164,11 @@
     sent_ref[...] = kept_ref[1] + received_ref[1]
 
 
-def prior_kernel(down_count, own_ref, kappa_ref, odd_ref, even_ref, prior_ref):
-    gx = lax.axis_index("gx")
-    held, rows, cols = own_ref.shape
+def prior_kernel(
+    scale, down_count, across, blocks_ref, own_ref, kappa_ref, mine_ref, odd_ref, even_ref, rest_ref, loadings_ref,
+):
+    gy, gx = lax.axis_index("gy"), lax.axis_index("gx")
     is_even = gx % 2 == 0
-    has_north = jnp.where(gx > 0, 1.0, 0.0)
-    has_south = jnp.where(gx < down_count - 1, 1.0, 0.0)
-    for k in range(held):
-        own, kappa = own_ref[k], kappa_ref[k]
-        above_edge = jnp.where(is_even, odd_ref[k], even_ref[k])
-        below_edge = jnp.where(is_even, even_ref[k], odd_ref[k])
-        once = operator(own, kappa, above_edge[:1], below_edge[:1], 0.0, 0.0)
-        above = (above_edge[1:] - own[:1]) * has_north
-        below = (below_edge[1:] - own[rows - 1:]) * has_south
-        prior_ref[k] = operator(once, kappa, above, below, 0.0, 0.0)
-
-
-def final_kernel(scale, down_count, across, blocks_ref, own_ref, kappa_ref, prior_ref, mine_ref, other_ref, latent_ref, loadings_ref):
-    gy, gx = lax.axis_index("gy"), lax.axis_index("gx")
     held, rows, cols = own_ref.shape
     fields, species = loadings_ref.shape
     per_row = LANES // species
@@ -219,13 +206,23 @@
         return jnp.where(col == edge, outer, 0.0) + jnp.where(col == inner, field, 0.0)
 
     for k in range(held):
-        latent_ref[k] = mine_ref[k] + other_ref[k] - prior_ref[k]
+        own, kappa = own_ref[k], kappa_ref[k]
+        above_edge = jnp.where(is_even, odd_ref[k], even_ref[k])
+        below_edge = jnp.where(is_even, even_ref[k], odd_ref[k])
+        once = operator(own, kappa, above_edge[:1], below_edge[:1], 0.0, 0.0)
+        above = (above_edge[1:] - own[:1]) * has_north
+        below = (below_edge[1:] - own[rows - 1:]) * has_south
+        rest_ref[k] = mine_ref[k] - operator(once, kappa, above, below, 0.0, 0.0)
         span = slice(0, LANES)
-        latent_ref[k, :, span] -= addition(
+        rest_ref[k, :, span] -= addition(
             k, west, span, own_ref[k, :, :1], kappa_ref[k, :, span], 0, 1, jnp.where(gy > 0, 1.0, 0.0))
         span = slice(cols - LANES, cols)
-        latent_ref[k, :, span] -= addition(
+        rest_ref[k, :, span] -= addition(
             k, east, span, own_ref[k, :, cols - 1:], kappa_ref[k, :, span], LANES - 1, LANES - 2, jnp.where(gy < across - 1, 1.0, 0.0))
+
+
+def final_kernel(rest_ref, other_ref, latent_ref):
+    latent_ref[...] = rest_ref[...] + other_ref[...]
 
 
 def per_device(latent, kappa_sq, coefs, loadings, counts, land):
@@ -279,22 +276,22 @@
         cost_estimate=pl.CostEstimate(flops=10**6, bytes_accessed=2**20, transcendentals=0),
     )(kept, received)
     other = lax.ppermute(sent, "sp", [(i, i ^ FAR) for i in range(groups)])
-    prior = pl.pallas_call(
-        functools.partial(prior_kernel, down_count),
-        in_specs=[vmem] * 4,
+    scale = 1.0 / math.sqrt(rows * down_count * cols * across)
+    rest, grad_loadings = pl.pallas_call(
+        functools.partial(prior_kernel, scale, down_count, across),
+        in_specs=[vmem] * 6,
+        out_specs=[vmem] * 2,
+        out_shape=[field_block, jax.ShapeDtypeStruct((fields, species), f32)],
+        compiler_params=params,
+        cost_estimate=pl.CostEstimate(flops=3*10**9, bytes_accessed=2**20, transcendentals=0),
+    )(blocks, own, kappa_sq, mine, by_odd, by_even)
+    grad_latent = pl.pallas_call(
+        final_kernel,
+        in_specs=[vmem] * 2,
         out_specs=vmem,
         out_shape=field_block,
         compiler_params=params,
-        cost_estimate=pl.CostEstimate(flops=3*10**9, bytes_accessed=2**20, transcendentals=0),
-    )(own, kappa_sq, by_odd, by_even)
-    scale = 1.0 / math.sqrt(rows * down_count * cols * across)
-    grad_latent, grad_loadings = pl.pallas_call(
-        functools.partial(final_kernel, scale, down_count, across),
-        in_specs=[vmem] * 6,
-        out_specs=[vmem, vmem],
-        out_shape=[field_block, jax.ShapeDtypeStruct((fields, species), f32)],
-        compiler_params=params,
-    )(blocks, own, kappa_sq, prior, mine, other)
+    )(rest, other)
     return grad_latent, grad_loadings.T
 
 

time: 43.3 us -> 42.7 us (0.986)
  waiting for transfers between devices: 3.74 us -> 2.87 us
    ppermute x1, waiting for transfers between devices: 3.73 us -> 2.86 us  [per_device(): other = lax.ppermute(sent, 'sp', [(i, i ^ FAR) for i in range(groups)])]
    pallas_call x2, Pallas kernels: 1.33 us -> 1.85 us  [the longest x1 1.18 us: per_device(): pl.pallas_call(functools.partial(prior_kernel, scale, down_count, across)...]
  transfers between devices with their start and end apart: 5 -> 5, of which waited for: 1 -> 1; matrix products, arithmetic and copies ran while one was open for 0% -> 0% of each run, Pallas kernels for 1% -> 3%
where the time goes in v5:
time: 42.7 us; the launch traced here: 42.4 us
  starting transfers between devices  33 us (77%)
  Pallas kernels  5.74 us (13%)
  waiting for transfers between devices  2.87 us (7%)
  between operations  0.81 us (2%)
    all_to_all x1, starting transfers between devices, per_device(): blocks = lax.all_to_all(blocks, ('gx', 'gy'), 0, 0, tiled=True)  17.5 us
    ppermute x2, starting transfers between devices, exchanged(): return lax.ppermute(edge, 'gx', pairs + [(j, i) for i, j in pairs])  7.96 us
    ppermute x1, starting transfers between devices, per_device(): other = lax.ppermute(sent, 'sp', [(i, i ^ FAR) for i in range(groups)])  4.13 us
    pallas_call x1, Pallas kernels, per_device(): pl.pallas_call(functools.partial(local_kernel, peers, across), in_specs=[...  3.87 us
    ppermute x1, starting transfers between devices, per_device(): received = lax.ppermute(sent, 'sp', [(i, i ^ NEAR) for i in range(groups)])  3.4 us
    ppermute x1, waiting for transfers between devices, per_device(): other = lax.ppermute(sent, 'sp', [(i, i ^ FAR) for i in range(groups)])  2.86 us
    pallas_call x1, Pallas kernels, per_device(): pl.pallas_call(functools.partial(prior_kernel, scale, down_count, across)...  1.18 us
  transfers between devices with their start and end apart: 5, of which 1 were waited for; matrix products, arithmetic and copies ran while one was open for 0% of the time, Pallas kernels for 3%

profile of v5, /device:TPU:40, one launch (start us, length us, event | category | flops | bytes accessed | tf_op | source)
XLA Modules:
  0.0 42.4 jit_solution(7451157014893586823)
XLA Ops:
  0.6 3.9 %shard_map.77 = (f32[128,5,1,128]{3,2,1,0:T(1,128)}, f32[4,16,512]{2,1,0:T(8,128)}, f32[4,2,512]{2,1,0:T(2,128)}, f32[4,2,512]{2,1,0:T(2,128)}, f32[2,4,16,512]{3,2,1,0:T(8,128)}, /*index=5*/f32[2,4,16,512]{3,2,1,0:T(8,128)}) custom-call(f32[16,32]{1,0:T(8,128)} %bitcast.2, f32[16,16,512]{2,1,0:T(8,128)} %latent_hbm.1, f32[4,16,512]{2,1,0:T(8,128)} %kappa_ref.1, ...), custom_call_target="tpu_custom_call" | custom-call | tf_op jit(solution)/shard_map/pallas_call | solution.py:242
  4.5 0.0 copy-start.3
  4.5 0.0 copy-start.5
  4.5 0.0 copy-start.4
  4.5 0.0 copy-start
  4.5 17.5 %all-to-all-start = ((f32[128,5,1,128]{3,2,1,0:T(1,128)}), f32[128,5,1,128]{3,2,1,0:T(1,128)S(1)}, u32[]{:S(2)}, u32[]{:S(2)}) async-start(f32[128,5,1,128]{3,2,1,0:T(1,128)} %get-tuple-element.12), calls=%async_computation | async-start | bytes 655360 | tf_op jit(solution)/shard_map/all_to_all | solution.py:261
  22.0 0.0 copy-done.3
  22.0 3.4 %collective-permute-start = (f32[2,4,16,512]{3,2,1,0:T(8,128)S(1)}, f32[2,4,16,512]{3,2,1,0:T(8,128)S(1)}, u32[]{:S(2)}, u32[]{:S(2)}) collective-permute-start(f32[2,4,16,512]{3,2,1,0:T(8,128)S(1)} %copy-done.3), channel_id=1, source_target_pairs={{0,1},{1,0},{2,3},{3,2},{4,5},{5,4},{6,7},{7,6},{8,9},{9,8},{10,11... | collective-permute-start | bytes 786440 | tf_op jit(solution)/shard_map/ppermute | solution.py:269
  25.4 0.0 copy-done.5
  25.5 6.0 %collective-permute-start.1 = (f32[4,2,512]{2,1,0:T(2,128)S(1)}, f32[4,2,512]{2,1,0:T(2,128)S(1)}, u32[]{:S(2)}, u32[]{:S(2)}) collective-permute-start(f32[4,2,512]{2,1,0:T(2,128)S(1)} %copy-done.5), channel_id=1, source_target_pairs={{16,32},{48,64},{80,96},{112,128},{144,160},{176,192},{208,224},{2... | collective-permute-start | bytes 49160 | tf_op jit(solution)/shard_map/ppermute | solution.py:265
  31.5 0.0 copy-done.4
  31.5 1.9 %collective-permute-start.2 = (f32[4,2,512]{2,1,0:T(2,128)S(1)}, f32[4,2,512]{2,1,0:T(2,128)S(1)}, u32[]{:S(2)}, u32[]{:S(2)}) collective-permute-start(f32[4,2,512]{2,1,0:T(2,128)S(1)} %copy-done.4), channel_id=1, source_target_pairs={{0,16},{32,48},{64,80},{96,112},{128,144},{160,176},{192,208},{224... | collective-permute-start | bytes 49160 | tf_op jit(solution)/shard_map/ppermute | solution.py:265
  33.4 0.0 collective-permute-done.received_ref
  33.5 0.0 copy-done
  33.5 0.0 copy-start.1
  33.5 0.0 copy-start.2
  33.5 4.1 %collective-permute-start.3 = (f32[4,16,512]{2,1,0:T(8,128)S(1)}, f32[4,16,512]{2,1,0:T(8,128)S(1)}, u32[]{:S(2)}, u32[]{:S(2)}) collective-permute-start(f32[4,16,512]{2,1,0:T(8,128)S(1)} %get-tuple-element.20), channel_id=1, source_target_pairs={{0,3},{1,2},{2,1},{3,0},{4,7},{5,6},{6,5},{7,4},{8,11},{9,10},{10,... | collective-permute-start | bytes 393224 | tf_op jit(solution)/shard_map/ppermute | solution.py:278
  37.7 0.0 collective-permute-done.1.odd_ref
  37.7 0.0 collective-permute-done.2.even_ref
  37.7 0.0 all-to-all-done.blocks_ref
  37.7 0.0 copy-done.1
  37.7 0.0 copy-done.2
  37.7 1.2 %shard_map.79 = (f32[4,16,512]{2,1,0:T(8,128)S(1)}, f32[16,32]{1,0:T(8,128)}) custom-call(f32[128,5,1,128]{3,2,1,0:T(1,128)S(1)} %all-to-all-done.blocks_ref, f32[4,16,512]{2,1,0:T(8,128)S(1)} %copy-done.2, f32[4,16,512]{2,1,0:T(8,128)S(1)} %copy-done.1, f32[4,16,512]{2,1,0:T(8,128)S(1)} %get-tuple-element.16.mine_ref, ...), custom_call_target="tpu_custom_call" | custom-call | flops 3000000000 | bytes 1048576 | tf_op jit(solution)/shard_map/pallas_call | solution.py:280
  38.9 2.9 %collective-permute-done.3.other_ref = f32[4,16,512]{2,1,0:T(8,128)S(1)} collective-permute-done((f32[4,16,512]{2,1,0:T(8,128)S(1)}, f32[4,16,512]{2,1,0:T(8,128)S(1)}, u32[]{:S(2)}, u32[]{:S(2)}) %collective-permute-start.3) | collective-permute-done | bytes 131104 | tf_op jit(solution)/shard_map/ppermute | solution.py:278
  41.8 0.7 %shard_map.80 = f32[4,16,512]{2,1,0:T(8,128)} custom-call(f32[4,16,512]{2,1,0:T(8,128)S(1)} %get-tuple-element.19.rest_ref, f32[4,16,512]{2,1,0:T(8,128)S(1)} %collective-permute-done.3.other_ref), custom_call_target="tpu_custom_call" | custom-call | tf_op jit(solution)/shard_map/pallas_call | solution.py:288
  (1 shorter events, 0.0 us)
Async XLA Ops:
  4.5 17.5 %copy-start.3 = (f32[2,4,16,512]{3,2,1,0:T(8,128)S(1)}, f32[2,4,16,512]{3,2,1,0:T(8,128)}, u32[]{:S(2)}) copy-start(f32[2,4,16,512]{3,2,1,0:T(8,128)} %get-tuple-element.15) | copy-start | bytes 786436
  4.5 20.9 %copy-start.5 = (f32[4,2,512]{2,1,0:T(2,128)S(1)}, f32[4,2,512]{2,1,0:T(2,128)}, u32[]{:S(2)}) copy-start(f32[4,2,512]{2,1,0:T(2,128)} %get-tuple-element.17) | copy-start | bytes 49156
  4.5 27.0 %copy-start.4 = (f32[4,2,512]{2,1,0:T(2,128)S(1)}, f32[4,2,512]{2,1,0:T(2,128)}, u32[]{:S(2)}) copy-start(f32[4,2,512]{2,1,0:T(2,128)} %get-tuple-element.18) | copy-start | bytes 49156
  4.5 28.9 %copy-start = (f32[2,4,16,512]{3,2,1,0:T(8,128)S(1)}, f32[2,4,16,512]{3,2,1,0:T(8,128)}, u32[]{:S(2)}) copy-start(f32[2,4,16,512]{3,2,1,0:T(8,128)} %get-tuple-element.14.kept_ref) | copy-start | bytes 786436
  4.5 33.1 %all-to-all-start = ((f32[128,5,1,128]{3,2,1,0:T(1,128)}), f32[128,5,1,128]{3,2,1,0:T(1,128)S(1)}, u32[]{:S(2)}, u32[]{:S(2)}) async-start(f32[128,5,1,128]{3,2,1,0:T(1,128)} %get-tuple-element.12), calls=%async_computation | async-start | bytes 655360 | tf_op jit(solution)/shard_map/all_to_all | solution.py:261
  22.0 11.4 %collective-permute-start = (f32[2,4,16,512]{3,2,1,0:T(8,128)S(1)}, f32[2,4,16,512]{3,2,1,0:T(8,128)S(1)}, u32[]{:S(2)}, u32[]{:S(2)}) collective-permute-start(f32[2,4,16,512]{3,2,1,0:T(8,128)S(1)} %copy-done.3), channel_id=1, source_target_pairs={{0,1},{1,0},{2,3},{3,2},{4,5},{5,4},{6,7},{7,6},{8,9},{9,8},{10,11... | collective-permute-start | bytes 786440 | tf_op jit(solution)/shard_map/ppermute | solution.py:269
  25.5 12.2 %collective-permute-start.1 = (f32[4,2,512]{2,1,0:T(2,128)S(1)}, f32[4,2,512]{2,1,0:T(2,128)S(1)}, u32[]{:S(2)}, u32[]{:S(2)}) collective-permute-start(f32[4,2,512]{2,1,0:T(2,128)S(1)} %copy-done.5), channel_id=1, source_target_pairs={{16,32},{48,64},{80,96},{112,128},{144,160},{176,192},{208,224},{2... | collective-permute-start | bytes 49160 | tf_op jit(solution)/shard_map/ppermute | solution.py:265
  31.5 6.2 %collective-permute-start.2 = (f32[4,2,512]{2,1,0:T(2,128)S(1)}, f32[4,2,512]{2,1,0:T(2,128)S(1)}, u32[]{:S(2)}, u32[]{:S(2)}) collective-permute-start(f32[4,2,512]{2,1,0:T(2,128)S(1)} %copy-done.4), channel_id=1, source_target_pairs={{0,16},{32,48},{64,80},{96,112},{128,144},{160,176},{192,208},{224... | collective-permute-start | bytes 49160 | tf_op jit(solution)/shard_map/ppermute | solution.py:265
  33.5 4.2 %copy-start.1 = (f32[4,16,512]{2,1,0:T(8,128)S(1)}, f32[4,16,512]{2,1,0:T(8,128)}, u32[]{:S(2)}) copy-start(f32[4,16,512]{2,1,0:T(8,128)} %kappa_ref.1) | copy-start | bytes 393220
  33.5 4.2 %copy-start.2 = (f32[4,16,512]{2,1,0:T(8,128)S(1)}, f32[4,16,512]{2,1,0:T(8,128)}, u32[]{:S(2)}) copy-start(f32[4,16,512]{2,1,0:T(8,128)} %get-tuple-element.13.own_ref) | copy-start | bytes 393220
  33.5 8.2 %collective-permute-start.3 = (f32[4,16,512]{2,1,0:T(8,128)S(1)}, f32[4,16,512]{2,1,0:T(8,128)S(1)}, u32[]{:S(2)}, u32[]{:S(2)}) collective-permute-start(f32[4,16,512]{2,1,0:T(8,128)S(1)} %get-tuple-element.20), channel_id=1, source_target_pairs={{0,3},{1,2},{2,1},{3,0},{4,7},{5,6},{6,5},{7,4},{8,11},{9,10},{10,... | collective-permute-start | bytes 393224 | tf_op jit(solution)/shard_map/ppermute | solution.py:278

commit v6 on v5

--- a/solution.py
+++ b/solution.py
@@ -219,10 +219,6 @@
         span = slice(cols - LANES, cols)
         rest_ref[k, :, span] -= addition(
             k, east, span, own_ref[k, :, cols - 1:], kappa_ref[k, :, span], LANES - 1, LANES - 2, jnp.where(gy < across - 1, 1.0, 0.0))
-
-
-def final_kernel(rest_ref, other_ref, latent_ref):
-    latent_ref[...] = rest_ref[...] + other_ref[...]
 
 
 def per_device(latent, kappa_sq, coefs, loadings, counts, land):
@@ -285,14 +281,7 @@
         compiler_params=params,
         cost_estimate=pl.CostEstimate(flops=3*10**9, bytes_accessed=2**20, transcendentals=0),
     )(blocks, own, kappa_sq, mine, by_odd, by_even)
-    grad_latent = pl.pallas_call(
-        final_kernel,
-        in_specs=[vmem] * 2,
-        out_specs=vmem,
-        out_shape=field_block,
-        compiler_params=params,
-    )(rest, other)
-    return grad_latent, grad_loadings.T
+    return rest + other, grad_loadings.T
 
 
 def solution(mesh):

time: 42.7 us -> 42.7 us (level)
  other arithmetic: 0 us -> 0.67 us
  Pallas kernels: 5.74 us -> 5.07 us
    add x0 -> x1, other arithmetic: none -> 0.67 us  [per_device(): return (rest + other, grad_loadings.T)]
    pallas_call x1 -> x0, Pallas kernels: 0.67 us -> none  [per_device(): pl.pallas_call(final_kernel, in_specs=[vmem] * 2, out_specs=vmem, out_sha...]
where the time goes in v6:
time: 42.7 us; the launch traced here: 42.4 us
  starting transfers between devices  33 us (77%)
  Pallas kernels  5.07 us (12%)
  waiting for transfers between devices  2.87 us (7%)
  between operations  0.81 us (2%)
  other arithmetic  0.67 us (2%)
    all_to_all x1, starting transfers between devices, per_device(): blocks = lax.all_to_all(blocks, ('gx', 'gy'), 0, 0, tiled=True)  17.5 us
    ppermute x2, starting transfers between devices, exchanged(): return lax.ppermute(edge, 'gx', pairs + [(j, i) for i, j in pairs])  7.96 us
    ppermute x1, starting transfers between devices, per_device(): other = lax.ppermute(sent, 'sp', [(i, i ^ FAR) for i in range(groups)])  4.13 us
    pallas_call x1, Pallas kernels, per_device(): pl.pallas_call(functools.partial(local_kernel, peers, across), in_specs=[...  3.87 us
    ppermute x1, starting transfers between devices, per_device(): received = lax.ppermute(sent, 'sp', [(i, i ^ NEAR) for i in range(groups)])  3.4 us
    ppermute x1, waiting for transfers between devices, per_device(): other = lax.ppermute(sent, 'sp', [(i, i ^ FAR) for i in range(groups)])  2.86 us
    pallas_call x1, Pallas kernels, per_device(): pl.pallas_call(functools.partial(prior_kernel, scale, down_count, across)...  1.18 us
  transfers between devices with their start and end apart: 5, of which 1 were waited for; matrix products, arithmetic and copies ran while one was open for 0% of the time, Pallas kernels for 3%

profile of v6, /device:TPU:40, one launch (start us, length us, event | category | flops | bytes accessed | tf_op | source)
XLA Modules:
  0.0 42.4 jit_solution(8744339712916458911)
XLA Ops:
  0.6 3.9 %shard_map.77 = (f32[128,5,1,128]{3,2,1,0:T(1,128)}, f32[4,16,512]{2,1,0:T(8,128)}, f32[4,2,512]{2,1,0:T(2,128)}, f32[4,2,512]{2,1,0:T(2,128)}, f32[2,4,16,512]{3,2,1,0:T(8,128)}, /*index=5*/f32[2,4,16,512]{3,2,1,0:T(8,128)}) custom-call(f32[16,32]{1,0:T(8,128)} %bitcast.2, f32[16,16,512]{2,1,0:T(8,128)} %latent_hbm.1, f32[4,16,512]{2,1,0:T(8,128)} %kappa_ref.1, ...), custom_call_target="tpu_custom_call" | custom-call | tf_op jit(solution)/shard_map/pallas_call | solution.py:238
  4.5 0.0 copy-start.3
  4.5 0.0 copy-start.5
  4.5 0.0 copy-start.4
  4.5 0.0 copy-start
  4.5 17.5 %all-to-all-start = ((f32[128,5,1,128]{3,2,1,0:T(1,128)}), f32[128,5,1,128]{3,2,1,0:T(1,128)S(1)}, u32[]{:S(2)}, u32[]{:S(2)}) async-start(f32[128,5,1,128]{3,2,1,0:T(1,128)} %get-tuple-element.12), calls=%async_computation | async-start | bytes 655360 | tf_op jit(solution)/shard_map/all_to_all | solution.py:257
  22.0 0.0 copy-done.3
  22.0 3.4 %collective-permute-start = (f32[2,4,16,512]{3,2,1,0:T(8,128)S(1)}, f32[2,4,16,512]{3,2,1,0:T(8,128)S(1)}, u32[]{:S(2)}, u32[]{:S(2)}) collective-permute-start(f32[2,4,16,512]{3,2,1,0:T(8,128)S(1)} %copy-done.3), channel_id=1, source_target_pairs={{0,1},{1,0},{2,3},{3,2},{4,5},{5,4},{6,7},{7,6},{8,9},{9,8},{10,11... | collective-permute-start | bytes 786440 | tf_op jit(solution)/shard_map/ppermute | solution.py:265
  25.4 0.0 copy-done.5
  25.5 6.0 %collective-permute-start.1 = (f32[4,2,512]{2,1,0:T(2,128)S(1)}, f32[4,2,512]{2,1,0:T(2,128)S(1)}, u32[]{:S(2)}, u32[]{:S(2)}) collective-permute-start(f32[4,2,512]{2,1,0:T(2,128)S(1)} %copy-done.5), channel_id=1, source_target_pairs={{16,32},{48,64},{80,96},{112,128},{144,160},{176,192},{208,224},{2... | collective-permute-start | bytes 49160 | tf_op jit(solution)/shard_map/ppermute | solution.py:261
  31.5 0.0 copy-done.4
  31.5 1.9 %collective-permute-start.2 = (f32[4,2,512]{2,1,0:T(2,128)S(1)}, f32[4,2,512]{2,1,0:T(2,128)S(1)}, u32[]{:S(2)}, u32[]{:S(2)}) collective-permute-start(f32[4,2,512]{2,1,0:T(2,128)S(1)} %copy-done.4), channel_id=1, source_target_pairs={{0,16},{32,48},{64,80},{96,112},{128,144},{160,176},{192,208},{224... | collective-permute-start | bytes 49160 | tf_op jit(solution)/shard_map/ppermute | solution.py:261
  33.4 0.0 collective-permute-done.received_ref
  33.5 0.0 copy-done
  33.5 0.0 copy-start.1
  33.5 0.0 copy-start.2
  33.5 4.1 %collective-permute-start.3 = (f32[4,16,512]{2,1,0:T(8,128)S(1)}, f32[4,16,512]{2,1,0:T(8,128)S(1)}, u32[]{:S(2)}, u32[]{:S(2)}) collective-permute-start(f32[4,16,512]{2,1,0:T(8,128)S(1)} %get-tuple-element.20), channel_id=1, source_target_pairs={{0,3},{1,2},{2,1},{3,0},{4,7},{5,6},{6,5},{7,4},{8,11},{9,10},{10,... | collective-permute-start | bytes 393224 | tf_op jit(solution)/shard_map/ppermute | solution.py:274
  37.7 0.0 collective-permute-done.1.odd_ref
  37.7 0.0 collective-permute-done.2.even_ref
  37.7 0.0 all-to-all-done.blocks_ref
  37.7 0.0 copy-done.1
  37.7 0.0 copy-done.2
  37.7 1.2 %shard_map.79 = (f32[4,16,512]{2,1,0:T(8,128)S(1)}, f32[16,32]{1,0:T(8,128)}) custom-call(f32[128,5,1,128]{3,2,1,0:T(1,128)S(1)} %all-to-all-done.blocks_ref, f32[4,16,512]{2,1,0:T(8,128)S(1)} %copy-done.2, f32[4,16,512]{2,1,0:T(8,128)S(1)} %copy-done.1, f32[4,16,512]{2,1,0:T(8,128)S(1)} %get-tuple-element.16.mine_ref, ...), custom_call_target="tpu_custom_call" | custom-call | flops 3000000000 | bytes 1048576 | tf_op jit(solution)/shard_map/pallas_call | solution.py:276
  38.9 2.9 %collective-permute-done.3 = f32[4,16,512]{2,1,0:T(8,128)S(1)} collective-permute-done((f32[4,16,512]{2,1,0:T(8,128)S(1)}, f32[4,16,512]{2,1,0:T(8,128)S(1)}, u32[]{:S(2)}, u32[]{:S(2)}) %collective-permute-start.3) | collective-permute-done | bytes 131104 | tf_op jit(solution)/shard_map/ppermute | solution.py:274
  41.8 0.7 %add.3 = f32[4,16,512]{2,1,0:T(8,128)} add(f32[4,16,512]{2,1,0:T(8,128)S(1)} %get-tuple-element.19, f32[4,16,512]{2,1,0:T(8,128)S(1)} %collective-permute-done.3) | non-fusion elementwise | flops 32768 | bytes 393216 | tf_op jit(solution)/shard_map/add | solution.py:284
  (1 shorter events, 0.0 us)
Async XLA Ops:
  4.5 17.5 %copy-start.3 = (f32[2,4,16,512]{3,2,1,0:T(8,128)S(1)}, f32[2,4,16,512]{3,2,1,0:T(8,128)}, u32[]{:S(2)}) copy-start(f32[2,4,16,512]{3,2,1,0:T(8,128)} %get-tuple-element.15) | copy-start | bytes 786436
  4.5 20.9 %copy-start.5 = (f32[4,2,512]{2,1,0:T(2,128)S(1)}, f32[4,2,512]{2,1,0:T(2,128)}, u32[]{:S(2)}) copy-start(f32[4,2,512]{2,1,0:T(2,128)} %get-tuple-element.17) | copy-start | bytes 49156
  4.5 27.0 %copy-start.4 = (f32[4,2,512]{2,1,0:T(2,128)S(1)}, f32[4,2,512]{2,1,0:T(2,128)}, u32[]{:S(2)}) copy-start(f32[4,2,512]{2,1,0:T(2,128)} %get-tuple-element.18) | copy-start | bytes 49156
  4.5 28.9 %copy-start = (f32[2,4,16,512]{3,2,1,0:T(8,128)S(1)}, f32[2,4,16,512]{3,2,1,0:T(8,128)}, u32[]{:S(2)}) copy-start(f32[2,4,16,512]{3,2,1,0:T(8,128)} %get-tuple-element.14.kept_ref) | copy-start | bytes 786436
  4.5 33.1 %all-to-all-start = ((f32[128,5,1,128]{3,2,1,0:T(1,128)}), f32[128,5,1,128]{3,2,1,0:T(1,128)S(1)}, u32[]{:S(2)}, u32[]{:S(2)}) async-start(f32[128,5,1,128]{3,2,1,0:T(1,128)} %get-tuple-element.12), calls=%async_computation | async-start | bytes 655360 | tf_op jit(solution)/shard_map/all_to_all | solution.py:257
  22.0 11.4 %collective-permute-start = (f32[2,4,16,512]{3,2,1,0:T(8,128)S(1)}, f32[2,4,16,512]{3,2,1,0:T(8,128)S(1)}, u32[]{:S(2)}, u32[]{:S(2)}) collective-permute-start(f32[2,4,16,512]{3,2,1,0:T(8,128)S(1)} %copy-done.3), channel_id=1, source_target_pairs={{0,1},{1,0},{2,3},{3,2},{4,5},{5,4},{6,7},{7,6},{8,9},{9,8},{10,11... | collective-permute-start | bytes 786440 | tf_op jit(solution)/shard_map/ppermute | solution.py:265
  25.5 12.2 %collective-permute-start.1 = (f32[4,2,512]{2,1,0:T(2,128)S(1)}, f32[4,2,512]{2,1,0:T(2,128)S(1)}, u32[]{:S(2)}, u32[]{:S(2)}) collective-permute-start(f32[4,2,512]{2,1,0:T(2,128)S(1)} %copy-done.5), channel_id=1, source_target_pairs={{16,32},{48,64},{80,96},{112,128},{144,160},{176,192},{208,224},{2... | collective-permute-start | bytes 49160 | tf_op jit(solution)/shard_map/ppermute | solution.py:261
  31.5 6.2 %collective-permute-start.2 = (f32[4,2,512]{2,1,0:T(2,128)S(1)}, f32[4,2,512]{2,1,0:T(2,128)S(1)}, u32[]{:S(2)}, u32[]{:S(2)}) collective-permute-start(f32[4,2,512]{2,1,0:T(2,128)S(1)} %copy-done.4), channel_id=1, source_target_pairs={{0,16},{32,48},{64,80},{96,112},{128,144},{160,176},{192,208},{224... | collective-permute-start | bytes 49160 | tf_op jit(solution)/shard_map/ppermute | solution.py:261
  33.5 4.2 %copy-start.1 = (f32[4,16,512]{2,1,0:T(8,128)S(1)}, f32[4,16,512]{2,1,0:T(8,128)}, u32[]{:S(2)}) copy-start(f32[4,16,512]{2,1,0:T(8,128)} %kappa_ref.1) | copy-start | bytes 393220
  33.5 4.2 %copy-start.2 = (f32[4,16,512]{2,1,0:T(8,128)S(1)}, f32[4,16,512]{2,1,0:T(8,128)}, u32[]{:S(2)}) copy-start(f32[4,16,512]{2,1,0:T(8,128)} %get-tuple-element.13.own_ref) | copy-start | bytes 393220
  33.5 8.2 %collective-permute-start.3 = (f32[4,16,512]{2,1,0:T(8,128)S(1)}, f32[4,16,512]{2,1,0:T(8,128)S(1)}, u32[]{:S(2)}, u32[]{:S(2)}) collective-permute-start(f32[4,16,512]{2,1,0:T(8,128)S(1)} %get-tuple-element.20), channel_id=1, source_target_pairs={{0,3},{1,2},{2,1},{3,0},{4,7},{5,6},{6,5},{7,4},{8,11},{9,10},{10,... | collective-permute-start | bytes 393224 | tf_op jit(solution)/shard_map/ppermute | solution.py:274

commit v7 on v6

--- a/solution.py
+++ b/solution.py
@@ -165,7 +165,7 @@
 
 
 def prior_kernel(
-    scale, down_count, across, blocks_ref, own_ref, kappa_ref, mine_ref, odd_ref, even_ref, rest_ref, loadings_ref,
+    scale, down_count, across, blocks_ref, own_ref, kappa_ref, mine_ref, even_ref, odd_ref, rest_ref, loadings_ref,
 ):
     gy, gx = lax.axis_index("gy"), lax.axis_index("gx")
     is_even = gx % 2 == 0
@@ -280,7 +280,7 @@
         out_shape=[field_block, jax.ShapeDtypeStruct((fields, species), f32)],
         compiler_params=params,
         cost_estimate=pl.CostEstimate(flops=3*10**9, bytes_accessed=2**20, transcendentals=0),
-    )(blocks, own, kappa_sq, mine, by_odd, by_even)
+    )(blocks, own, kappa_sq, mine, by_even, by_odd)
     return rest + other, grad_loadings.T
 
 

time: 42.7 us -> 43.2 us (1.012)
  starting transfers between devices: 33 us -> 33.5 us
    ppermute x2, starting transfers between devices: 7.96 us -> 8.48 us  [exchanged(): return lax.ppermute(edge, 'gx', pairs + [(j, i) for i, j in pairs])]
where the time goes in v7:
time: 43.2 us; the launch traced here: 42.9 us
  starting transfers between devices  33.5 us (78%)
  Pallas kernels  5.07 us (12%)
  waiting for transfers between devices  2.84 us (7%)
  between operations  0.81 us (2%)
  other arithmetic  0.67 us (2%)
    all_to_all x1, starting transfers between devices, per_device(): blocks = lax.all_to_all(blocks, ('gx', 'gy'), 0, 0, tiled=True)  17.5 us
    ppermute x2, starting transfers between devices, exchanged(): return lax.ppermute(edge, 'gx', pairs + [(j, i) for i, j in pairs])  8.48 us
    ppermute x1, starting transfers between devices, per_device(): other = lax.ppermute(sent, 'sp', [(i, i ^ FAR) for i in range(groups)])  4.13 us
    pallas_call x1, Pallas kernels, per_device(): pl.pallas_call(functools.partial(local_kernel, peers, across), in_specs=[...  3.87 us
    ppermute x1, starting transfers between devices, per_device(): received = lax.ppermute(sent, 'sp', [(i, i ^ NEAR) for i in range(groups)])  3.4 us
    ppermute x1, waiting for transfers between devices, per_device(): other = lax.ppermute(sent, 'sp', [(i, i ^ FAR) for i in range(groups)])  2.83 us
    pallas_call x1, Pallas kernels, per_device(): pl.pallas_call(functools.partial(prior_kernel, scale, down_count, across)...  1.18 us
  transfers between devices with their start and end apart: 5, of which 1 were waited for; matrix products, arithmetic and copies ran while one was open for 0% of the time, Pallas kernels for 3%

profile of v7, /device:TPU:40, one launch (start us, length us, event | category | flops | bytes accessed | tf_op | source)
XLA Modules:
  0.0 42.9 jit_solution(10987966042984393020)
XLA Ops:
  0.6 3.9 %shard_map.77 = (f32[128,5,1,128]{3,2,1,0:T(1,128)}, f32[4,16,512]{2,1,0:T(8,128)}, f32[4,2,512]{2,1,0:T(2,128)}, f32[4,2,512]{2,1,0:T(2,128)}, f32[2,4,16,512]{3,2,1,0:T(8,128)}, /*index=5*/f32[2,4,16,512]{3,2,1,0:T(8,128)}) custom-call(f32[16,32]{1,0:T(8,128)} %bitcast.2, f32[16,16,512]{2,1,0:T(8,128)} %latent_hbm.1, f32[4,16,512]{2,1,0:T(8,128)} %kappa_ref.1, ...), custom_call_target="tpu_custom_call" | custom-call | tf_op jit(solution)/shard_map/pallas_call | solution.py:238
  4.5 0.0 copy-start.3
  4.5 0.0 copy-start.5
  4.5 0.0 copy-start.4
  4.5 0.0 copy-start
  4.5 17.5 %all-to-all-start = ((f32[128,5,1,128]{3,2,1,0:T(1,128)}), f32[128,5,1,128]{3,2,1,0:T(1,128)S(1)}, u32[]{:S(2)}, u32[]{:S(2)}) async-start(f32[128,5,1,128]{3,2,1,0:T(1,128)} %get-tuple-element.12), calls=%async_computation | async-start | bytes 655360 | tf_op jit(solution)/shard_map/all_to_all | solution.py:257
  22.0 0.0 copy-done.3
  22.0 3.4 %collective-permute-start = (f32[2,4,16,512]{3,2,1,0:T(8,128)S(1)}, f32[2,4,16,512]{3,2,1,0:T(8,128)S(1)}, u32[]{:S(2)}, u32[]{:S(2)}) collective-permute-start(f32[2,4,16,512]{3,2,1,0:T(8,128)S(1)} %copy-done.3), channel_id=1, source_target_pairs={{0,1},{1,0},{2,3},{3,2},{4,5},{5,4},{6,7},{7,6},{8,9},{9,8},{10,11... | collective-permute-start | bytes 786440 | tf_op jit(solution)/shard_map/ppermute | solution.py:265
  25.4 0.0 copy-done.5
  25.5 3.4 %collective-permute-start.1 = (f32[4,2,512]{2,1,0:T(2,128)S(1)}, f32[4,2,512]{2,1,0:T(2,128)S(1)}, u32[]{:S(2)}, u32[]{:S(2)}) collective-permute-start(f32[4,2,512]{2,1,0:T(2,128)S(1)} %copy-done.5), channel_id=1, source_target_pairs={{0,16},{32,48},{64,80},{96,112},{128,144},{160,176},{192,208},{224... | collective-permute-start | bytes 49160 | tf_op jit(solution)/shard_map/ppermute | solution.py:261
  28.9 0.0 copy-done.4
  28.9 5.1 %collective-permute-start.2 = (f32[4,2,512]{2,1,0:T(2,128)S(1)}, f32[4,2,512]{2,1,0:T(2,128)S(1)}, u32[]{:S(2)}, u32[]{:S(2)}) collective-permute-start(f32[4,2,512]{2,1,0:T(2,128)S(1)} %copy-done.4), channel_id=1, source_target_pairs={{16,32},{48,64},{80,96},{112,128},{144,160},{176,192},{208,224},{2... | collective-permute-start | bytes 49160 | tf_op jit(solution)/shard_map/ppermute | solution.py:261
  34.0 0.0 collective-permute-done.received_ref
  34.0 0.0 copy-done
  34.0 0.0 copy-start.1
  34.0 0.0 copy-start.2
  34.1 4.1 %collective-permute-start.3 = (f32[4,16,512]{2,1,0:T(8,128)S(1)}, f32[4,16,512]{2,1,0:T(8,128)S(1)}, u32[]{:S(2)}, u32[]{:S(2)}) collective-permute-start(f32[4,16,512]{2,1,0:T(8,128)S(1)} %get-tuple-element.20), channel_id=1, source_target_pairs={{0,3},{1,2},{2,1},{3,0},{4,7},{5,6},{6,5},{7,4},{8,11},{9,10},{10,... | collective-permute-start | bytes 393224 | tf_op jit(solution)/shard_map/ppermute | solution.py:274
  38.2 0.0 collective-permute-done.1.even_ref
  38.2 0.0 collective-permute-done.2.odd_ref
  38.2 0.0 all-to-all-done.blocks_ref
  38.2 0.0 copy-done.1
  38.2 0.0 copy-done.2
  38.2 1.2 %shard_map.79 = (f32[4,16,512]{2,1,0:T(8,128)S(1)}, f32[16,32]{1,0:T(8,128)}) custom-call(f32[128,5,1,128]{3,2,1,0:T(1,128)S(1)} %all-to-all-done.blocks_ref, f32[4,16,512]{2,1,0:T(8,128)S(1)} %copy-done.2, f32[4,16,512]{2,1,0:T(8,128)S(1)} %copy-done.1, f32[4,16,512]{2,1,0:T(8,128)S(1)} %get-tuple-element.16.mine_ref, ...), custom_call_target="tpu_custom_call" | custom-call | flops 3000000000 | bytes 1048576 | tf_op jit(solution)/shard_map/pallas_call | solution.py:276
  39.4 2.8 %collective-permute-done.3 = f32[4,16,512]{2,1,0:T(8,128)S(1)} collective-permute-done((f32[4,16,512]{2,1,0:T(8,128)S(1)}, f32[4,16,512]{2,1,0:T(8,128)S(1)}, u32[]{:S(2)}, u32[]{:S(2)}) %collective-permute-start.3) | collective-permute-done | bytes 131104 | tf_op jit(solution)/shard_map/ppermute | solution.py:274
  42.3 0.7 %add.3 = f32[4,16,512]{2,1,0:T(8,128)} add(f32[4,16,512]{2,1,0:T(8,128)S(1)} %get-tuple-element.19, f32[4,16,512]{2,1,0:T(8,128)S(1)} %collective-permute-done.3) | non-fusion elementwise | flops 32768 | bytes 393216 | tf_op jit(solution)/shard_map/add | solution.py:284
  (1 shorter events, 0.0 us)
Async XLA Ops:
  4.5 17.5 %copy-start.3 = (f32[2,4,16,512]{3,2,1,0:T(8,128)S(1)}, f32[2,4,16,512]{3,2,1,0:T(8,128)}, u32[]{:S(2)}) copy-start(f32[2,4,16,512]{3,2,1,0:T(8,128)} %get-tuple-element.15) | copy-start | bytes 786436
  4.5 20.9 %copy-start.5 = (f32[4,2,512]{2,1,0:T(2,128)S(1)}, f32[4,2,512]{2,1,0:T(2,128)}, u32[]{:S(2)}) copy-start(f32[4,2,512]{2,1,0:T(2,128)} %get-tuple-element.17) | copy-start | bytes 49156
  4.5 24.3 %copy-start.4 = (f32[4,2,512]{2,1,0:T(2,128)S(1)}, f32[4,2,512]{2,1,0:T(2,128)}, u32[]{:S(2)}) copy-start(f32[4,2,512]{2,1,0:T(2,128)} %get-tuple-element.18) | copy-start | bytes 49156
  4.5 29.4 %copy-start = (f32[2,4,16,512]{3,2,1,0:T(8,128)S(1)}, f32[2,4,16,512]{3,2,1,0:T(8,128)}, u32[]{:S(2)}) copy-start(f32[2,4,16,512]{3,2,1,0:T(8,128)} %get-tuple-element.14.kept_ref) | copy-start | bytes 786436
  4.5 33.7 %all-to-all-start = ((f32[128,5,1,128]{3,2,1,0:T(1,128)}), f32[128,5,1,128]{3,2,1,0:T(1,128)S(1)}, u32[]{:S(2)}, u32[]{:S(2)}) async-start(f32[128,5,1,128]{3,2,1,0:T(1,128)} %get-tuple-element.12), calls=%async_computation | async-start | bytes 655360 | tf_op jit(solution)/shard_map/all_to_all | solution.py:257
  22.0 11.9 %collective-permute-start = (f32[2,4,16,512]{3,2,1,0:T(8,128)S(1)}, f32[2,4,16,512]{3,2,1,0:T(8,128)S(1)}, u32[]{:S(2)}, u32[]{:S(2)}) collective-permute-start(f32[2,4,16,512]{3,2,1,0:T(8,128)S(1)} %copy-done.3), channel_id=1, source_target_pairs={{0,1},{1,0},{2,3},{3,2},{4,5},{5,4},{6,7},{7,6},{8,9},{9,8},{10,11... | collective-permute-start | bytes 786440 | tf_op jit(solution)/shard_map/ppermute | solution.py:265
  25.5 12.7 %collective-permute-start.1 = (f32[4,2,512]{2,1,0:T(2,128)S(1)}, f32[4,2,512]{2,1,0:T(2,128)S(1)}, u32[]{:S(2)}, u32[]{:S(2)}) collective-permute-start(f32[4,2,512]{2,1,0:T(2,128)S(1)} %copy-done.5), channel_id=1, source_target_pairs={{0,16},{32,48},{64,80},{96,112},{128,144},{160,176},{192,208},{224... | collective-permute-start | bytes 49160 | tf_op jit(solution)/shard_map/ppermute | solution.py:261
  28.9 9.3 %collective-permute-start.2 = (f32[4,2,512]{2,1,0:T(2,128)S(1)}, f32[4,2,512]{2,1,0:T(2,128)S(1)}, u32[]{:S(2)}, u32[]{:S(2)}) collective-permute-start(f32[4,2,512]{2,1,0:T(2,128)S(1)} %copy-done.4), channel_id=1, source_target_pairs={{16,32},{48,64},{80,96},{112,128},{144,160},{176,192},{208,224},{2... | collective-permute-start | bytes 49160 | tf_op jit(solution)/shard_map/ppermute | solution.py:261
  34.0 4.2 %copy-start.1 = (f32[4,16,512]{2,1,0:T(8,128)S(1)}, f32[4,16,512]{2,1,0:T(8,128)}, u32[]{:S(2)}) copy-start(f32[4,16,512]{2,1,0:T(8,128)} %kappa_ref.1) | copy-start | bytes 393220
  34.0 4.2 %copy-start.2 = (f32[4,16,512]{2,1,0:T(8,128)S(1)}, f32[4,16,512]{2,1,0:T(8,128)}, u32[]{:S(2)}) copy-start(f32[4,16,512]{2,1,0:T(8,128)} %get-tuple-element.13.own_ref) | copy-start | bytes 393220
  34.1 8.2 %collective-permute-start.3 = (f32[4,16,512]{2,1,0:T(8,128)S(1)}, f32[4,16,512]{2,1,0:T(8,128)S(1)}, u32[]{:S(2)}, u32[]{:S(2)}) collective-permute-start(f32[4,16,512]{2,1,0:T(8,128)S(1)} %get-tuple-element.20), channel_id=1, source_target_pairs={{0,3},{1,2},{2,1},{3,0},{4,7},{5,6},{6,5},{7,4},{8,11},{9,10},{10,... | collective-permute-start | bytes 393224 | tf_op jit(solution)/shard_map/ppermute | solution.py:274
